TPU v7x, 256 devices: a whole 4x4x8 slice. The times are simulated.
256 devices in a mesh: fsdp: 64 (over x, z, core), mp: 4 (over y).
Axes of the slice: x: 4, y: 4, z: 8, core: 2. Of those that a mesh axis runs over, the one named last changes fastest.
Arguments:
- gradient: bfloat16 [4096, 14336], P('fsdp', 'mp')
- first_moment: float32 [4096, 14336], P('fsdp', 'mp'), may hold values from -4 to 4
- left_gram: float32 [64, 4, 512, 512], P('fsdp', 'mp')
- right_gram: float32 [64, 4, 512, 512], P('fsdp', 'mp')
- left_basis: bfloat16 [64, 4, 512, 512], P('fsdp', 'mp'), may hold values from -0.25 to 0.25
- right_basis: bfloat16 [64, 4, 512, 512], P('fsdp', 'mp'), may hold values from -0.25 to 0.25
- second_moment: float32 [64, 4, 512, 512], P('fsdp', 'mp'), may hold values from 0.02 to 0.2
- block_target: int32 [4, 56], P('mp'), may hold values from 0 to 63, as said below
Outputs:
- param_update: bfloat16 [4096, 14336], P('fsdp', 'mp')
- first_next: float32 [4096, 14336], P('fsdp', 'mp')
- left_next: float32 [64, 4, 512, 512], P('fsdp', 'mp')
- right_next: float32 [64, 4, 512, 512], P('fsdp', 'mp')
- second_next: float32 [64, 4, 512, 512], P('fsdp', 'mp')
Inputs may be any that keep to these rules, and one draw needn't show every extreme that they name: `block_target`: A value names the fsdp owner of a block. Values within one row are distinct.
All inputs are finite; a program needn't handle non-finite values.
Results may differ from a plain program's by a relative error of at most 0.0061.
Values may be sent and summed in bfloat16 or wider, within the bound.
A program may use at most 64 MiB of HBM per device.

v0:
```python
import jax
import jax.numpy as jnp
from jax import lax
from jax.sharding import PartitionSpec as P

CLIP_RMS = 0.5
FIRST_DECAY = 0.9
GRAM_DECAY = 0.95
GRAM_RATE = 0.05
SECOND_DECAY = 0.95
SECOND_RATE = 0.05
EPSILON = 1e-08


def shards(
    gradient,
    first_moment,
    left_gram,
    right_gram,
    left_basis,
    right_basis,
    second_moment,
    block_target,
):
    row_count, col_count = gradient.shape
    block_size = left_gram.shape[-1]
    owner_count = lax.axis_size("fsdp")
    group_count = lax.axis_size("mp")
    my_index = lax.axis_index("fsdp")
    band_devices = block_size // row_count
    band_count = owner_count // band_devices
    block_columns = col_count // block_size
    my_band = my_index // band_devices
    listing = block_target[0]
    my_targets = lax.dynamic_slice_in_dim(listing, my_band * block_columns, block_columns)
    owner_ids = jnp.arange(owner_count, dtype=jnp.int32)
    band_ids = jnp.arange(band_count, dtype=jnp.int32)
    owner_hits = listing == my_index
    owner_live = jnp.any(owner_hits)
    block_band = jnp.arange(listing.shape[0], dtype=jnp.int32) // block_columns
    owner_band = jnp.sum(jnp.where(owner_hits, block_band, 0))
    band_pick = ((band_ids == owner_band) & owner_live).astype(jnp.bfloat16)
    to_owner = (my_targets[:, None] == owner_ids[None, :]).astype(jnp.bfloat16)
    grad_pieces = gradient.reshape(row_count, block_columns, block_size)
    sent_grad = jnp.einsum(
        "jo,rjc->orc", to_owner, grad_pieces, preferred_element_type=jnp.float32
    ).astype(jnp.bfloat16)
    grad_wide = gradient.astype(jnp.float32)
    norm_sum = lax.psum(jnp.sum(grad_wide * grad_wide), ("fsdp", "mp"))
    clip_factor = jnp.minimum(
        1.0,
        CLIP_RMS
        * jnp.sqrt(float(row_count * owner_count * col_count * group_count))
        / jnp.sqrt(norm_sum),
    )
    first_next = FIRST_DECAY * first_moment + (1.0 - FIRST_DECAY) * clip_factor * grad_wide
    moment = first_next.astype(jnp.bfloat16)
    moment_pieces = moment.reshape(row_count, block_columns, block_size)
    sent_moment = jnp.einsum(
        "jo,rjc->orc", to_owner, moment_pieces, preferred_element_type=jnp.float32
    ).astype(jnp.bfloat16)
    came_grad, came_moment = (
        lax.all_to_all(sent_grad, "fsdp", split_axis=0, concat_axis=0, tiled=True),
        lax.all_to_all(sent_moment, "fsdp", split_axis=0, concat_axis=0, tiled=True),
    )
    block = lax.dynamic_slice_in_dim(came_grad, owner_band * band_devices, band_devices, 0).reshape(
        block_size, block_size
    )
    moment_block = lax.dynamic_slice_in_dim(
        came_moment, owner_band * band_devices, band_devices, 0
    ).reshape(block_size, block_size)
    left_mat = left_basis[0, 0]
    right_mat = right_basis[0, 0]
    gram_scale = GRAM_RATE * clip_factor * clip_factor / block_size
    gram_left = jnp.dot(block, block.T, preferred_element_type=jnp.float32)
    gram_right = jnp.dot(block.T, block, preferred_element_type=jnp.float32)
    left_next = jnp.where(
        owner_live, GRAM_DECAY * left_gram[0, 0] + gram_scale * gram_left, left_gram[0, 0]
    )
    right_next = jnp.where(
        owner_live, GRAM_DECAY * right_gram[0, 0] + gram_scale * gram_right, right_gram[0, 0]
    )
    left_half = jnp.dot(left_mat.T, block, preferred_element_type=jnp.float32).astype(jnp.bfloat16)
    rotated = clip_factor * jnp.dot(left_half, right_mat, preferred_element_type=jnp.float32)
    fresh_second = SECOND_DECAY * second_moment[0, 0] + SECOND_RATE * rotated * rotated
    second_next = jnp.where(owner_live, fresh_second, second_moment[0, 0])
    moment_half = jnp.dot(left_mat.T, moment_block, preferred_element_type=jnp.float32).astype(
        jnp.bfloat16
    )
    moment_rot = jnp.dot(moment_half, right_mat, preferred_element_type=jnp.float32)
    normed = (moment_rot / (jnp.sqrt(fresh_second) + EPSILON)).astype(jnp.bfloat16)
    back_half = jnp.dot(left_mat, normed, preferred_element_type=jnp.float32).astype(jnp.bfloat16)
    owner_update = jnp.dot(back_half, right_mat.T, preferred_element_type=jnp.float32).astype(
        jnp.bfloat16
    )
    owner_pieces = owner_update.reshape(band_devices, row_count, block_size)
    back_rows = band_pick[:, None, None, None] * owner_pieces[None]
    back_rows = back_rows.reshape(owner_count, row_count, block_size)
    came_back = lax.all_to_all(back_rows, "fsdp", split_axis=0, concat_axis=0, tiled=True)
    param_update = jnp.einsum(
        "jo,orc->rjc", to_owner, came_back, preferred_element_type=jnp.float32
    ).astype(jnp.bfloat16)
    param_update = param_update.reshape(row_count, col_count)
    return (
        param_update,
        first_next,
        left_next[None, None],
        right_next[None, None],
        second_next[None, None],
    )


def solution(mesh):
    return jax.shard_map(
        shards,
        mesh=mesh,
        in_specs=(
            P("fsdp", "mp"),
            P("fsdp", "mp"),
            P("fsdp", "mp", None, None),
            P("fsdp", "mp", None, None),
            P("fsdp", "mp", None, None),
            P("fsdp", "mp", None, None),
            P("fsdp", "mp", None, None),
            P("mp", None),
        ),
        out_specs=(
            P("fsdp", "mp"),
            P("fsdp", "mp"),
            P("fsdp", "mp", None, None),
            P("fsdp", "mp", None, None),
            P("fsdp", "mp", None, None),
        ),
        check_vma=False,
    )
```

profile of v0, /device:TPU:1, one launch (start us, length us, event | category | flops | bytes accessed | tf_op | source)
XLA Modules:
  0.0 391.9 jit_solution(149376673999545159)
XLA Ops:
  0.6 0.0 copy-start
  0.7 1.6 reshape.42
  2.3 0.7 fusion.34
  3.0 1.4 convolution_convert_fusion
  4.4 4.3 %copy.22 = bf16[64,64,512]{2,1,0:T(8,128)(2,1)} copy(bf16[64,64,512]{2,0,1:T(8,128)(2,1)S(1)} %convolution_convert_fusion) | data formatting | bytes 8388608 | tf_op jit(solution)/shard_map/convert_element_type | solution.py:47
  8.7 13.3 %all-to-all-start.1 = ((bf16[64,64,512]{2,1,0:T(8,128)(2,1)}), bf16[64,64,512]{2,1,0:T(8,128)(2,1)}, u32[]{:S(2)}, u32[]{:S(2)}) async-start(bf16[64,64,512]{2,1,0:T(8,128)(2,1)} %copy.22), calls=%async_computation.1 | async-start | bytes 8388608 | tf_op jit(solution)/shard_map/all_to_all | solution.py:63
  22.1 0.8 fusion.15
  22.9 136.8 %psum.7 = f32[]{:T(128)} all-reduce(f32[]{:T(128)} %fusion.15), channel_id=1, replica_groups=mesh['fsdp'=64,'mp'=4] {'fsdp','mp'}, use_global_device_ids=true, to_apply=%region_3.4 | all-reduce | flops 1 | bytes 8 | tf_op jit(solution)/shard_map/psum | solution.py:49
  160.4 1.1 fusion.36
  161.5 0.5 reshape.40
  162.0 1.4 convolution_convert_fusion.1
  163.4 4.4 %copy.21 = bf16[64,64,512]{2,1,0:T(8,128)(2,1)} copy(bf16[64,64,512]{2,0,1:T(8,128)(2,1)S(1)} %convolution_convert_fusion.1) | data formatting | bytes 8388608 | tf_op jit(solution)/shard_map/convert_element_type | solution.py:61
  167.7 9.7 %all-to-all-start = ((bf16[64,64,512]{2,1,0:T(8,128)(2,1)}), bf16[64,64,512]{2,1,0:T(8,128)(2,1)}, u32[]{:S(2)}, u32[]{:S(2)}) async-start(bf16[64,64,512]{2,1,0:T(8,128)(2,1)} %copy.21), calls=%async_computation | async-start | bytes 8388608 | tf_op jit(solution)/shard_map/all_to_all | solution.py:64
  177.5 0.6 fusion.35
  178.8 0.7 compare_reduce_fusion
  179.4 1.3 and_convert_fusion
  180.7 0.1 mul.84
  180.8 0.1 mul.85
  180.9 1.1 constant_dynamic-slice_fusion
  182.0 1.9 fusion.6
  183.9 89.4 %all-to-all-done = bf16[64,64,512]{2,1,0:T(8,128)(2,1)} async-done(((bf16[64,64,512]{2,1,0:T(8,128)(2,1)}), bf16[64,64,512]{2,1,0:T(8,128)(2,1)}, u32[]{:S(2)}, u32[]{:S(2)}) %all-to-all-start) | async-done | bytes 4194336 | tf_op jit(solution)/shard_map/all_to_all | solution.py:64
  273.3 1.9 constant_dynamic-slice_fusion.1
  275.2 3.0 fusion.10
  278.2 2.9 convolution_convert_fusion.2
  281.1 3.4 bitcast_multiply_fusion
  284.5 6.1 %all-to-all-start.2 = ((bf16[64,64,512]{2,1,0:T(8,128)(2,1)}), bf16[64,64,512]{2,1,0:T(8,128)(2,1)}, u32[]{:S(2)}, u32[]{:S(2)}) async-start(bf16[64,64,512]{2,1,0:T(8,128)(2,1)} %bitcast_multiply_fusion), calls=%async_computation.2 | async-start | bytes 8388608 | tf_op jit(solution)/shard_map/all_to_all | solution.py:99
  290.6 2.2 fusion.5
  292.8 3.0 fusion.14
  295.8 2.4 fusion.9
  298.2 88.3 %all-to-all-done.2 = bf16[64,64,512]{2,1,0:T(8,128)(2,1)} async-done(((bf16[64,64,512]{2,1,0:T(8,128)(2,1)}), bf16[64,64,512]{2,1,0:T(8,128)(2,1)}, u32[]{:S(2)}, u32[]{:S(2)}) %all-to-all-start.2) | async-done | bytes 4194336 | tf_op jit(solution)/shard_map/all_to_all | solution.py:99
  386.5 4.5 %fusion.11 = bf16[64,512,7]{1,2,0:T(8,128)(2,1)S(1)} fusion(bf16[64,64,512]{2,1,0:T(8,128)(2,1)} %all-to-all-done.2, s32[7]{0:T(128)S(1)} %fusion.34), kind=kOutput, calls=%fused_computation.23 | convolution fusion | flops 29589952 | bytes 4653084 | tf_op jit(solution)/shard_map/jo,orc->rjc/dot_general | solution.py:100
  391.0 0.9 copy.27
  (16 shorter events, 0.0 us)
Async XLA Ops:
  0.6 181.3 %copy-start = (bf16[1,1,512,512]{3,2,1,0:T(8,128)(2,1)S(1)}, bf16[1,1,512,512]{3,2,1,0:T(8,128)(2,1)}, u32[]{:S(2)}) copy-start(bf16[1,1,512,512]{3,2,1,0:T(8,128)(2,1)} %param.13) | copy-start | bytes 1572868
  8.7 13.3 %copy-start.1 = (bf16[64,3584]{1,0:T(8,128)(2,1)S(1)}, bf16[64,3584]{1,0:T(8,128)(2,1)}, u32[]{:S(2)}) copy-start(bf16[64,3584]{1,0:T(8,128)(2,1)} %param.8) | copy-start | bytes 1376260
  8.7 151.6 %copy-start.5 = (f32[64,3584]{1,0:T(8,128)S(1)}, f32[64,3584]{1,0:T(8,128)}, u32[]{:S(2)}) copy-start(f32[64,3584]{1,0:T(8,128)} %param.9) | copy-start | bytes 2752516
  8.7 159.0 %all-to-all-start.1 = ((bf16[64,64,512]{2,1,0:T(8,128)(2,1)}), bf16[64,64,512]{2,1,0:T(8,128)(2,1)}, u32[]{:S(2)}, u32[]{:S(2)}) async-start(bf16[64,64,512]{2,1,0:T(8,128)(2,1)} %copy.22), calls=%async_computation.1 | async-start | bytes 8388608 | tf_op jit(solution)/shard_map/all_to_all | solution.py:63
  167.7 9.7 %copy-start.7 = (s32[1,56]{1,0:T(1,128)S(1)}, s32[1,56]{1,0:T(1,128)}, u32[]{:S(2)}) copy-start(s32[1,56]{1,0:T(1,128)} %param.15) | copy-start | bytes 676
  167.7 14.2 %copy-start.3 = (f32[1,1,512,512]{3,2,1,0:T(8,128)S(1)}, f32[1,1,512,512]{3,2,1,0:T(8,128)}, u32[]{:S(2)}) copy-start(f32[1,1,512,512]{3,2,1,0:T(8,128)} %param.14) | copy-start | bytes 3145732
  167.7 105.6 %all-to-all-start = ((bf16[64,64,512]{2,1,0:T(8,128)(2,1)}), bf16[64,64,512]{2,1,0:T(8,128)(2,1)}, u32[]{:S(2)}, u32[]{:S(2)}) async-start(bf16[64,64,512]{2,1,0:T(8,128)(2,1)} %copy.21), calls=%async_computation | async-start | bytes 8388608 | tf_op jit(solution)/shard_map/all_to_all | solution.py:64
  183.9 97.1 %copy-start.4 = (f32[512,512]{1,0:T(8,128)}, f32[512,512]{1,0:T(8,128)S(1)}, u32[]{:S(2)}) copy-start(f32[512,512]{1,0:T(8,128)S(1)} %fusion.6) | copy-start | bytes 3145732
  284.5 6.1 %copy-start.2 = (f32[1,1,512,512]{3,2,1,0:T(8,128)S(1)}, f32[1,1,512,512]{3,2,1,0:T(8,128)}, u32[]{:S(2)}) copy-start(f32[1,1,512,512]{3,2,1,0:T(8,128)} %param.10) | copy-start | bytes 3145732
  284.5 102.0 %all-to-all-start.2 = ((bf16[64,64,512]{2,1,0:T(8,128)(2,1)}), bf16[64,64,512]{2,1,0:T(8,128)(2,1)}, u32[]{:S(2)}, u32[]{:S(2)}) async-start(bf16[64,64,512]{2,1,0:T(8,128)(2,1)} %bitcast_multiply_fusion), calls=%async_computation.2 | async-start | bytes 8388608 | tf_op jit(solution)/shard_map/all_to_all | solution.py:99
  290.6 5.2 %copy-start.6 = (f32[1,1,512,512]{3,2,1,0:T(8,128)S(1)}, f32[1,1,512,512]{3,2,1,0:T(8,128)}, u32[]{:S(2)}) copy-start(f32[1,1,512,512]{3,2,1,0:T(8,128)} %param.11) | copy-start | bytes 3145732
where the time goes:
time: 393 us; the launch traced here: 392 us
  waiting for transfers between devices  178 us (45%)
  blocking collectives  137 us (35%)
  starting transfers between devices  29.1 us (7%)
  matrix products  19.6 us (5%)
  local copies, waits for them, and re-layouts  15.7 us (4%)
  other arithmetic  11 us (3%)
    psum x1, blocking collectives, shards(): norm_sum = lax.psum(jnp.sum(grad_wide * grad_wide), ('fsdp', 'mp'))  137 us
    all_to_all x1, waiting for transfers between devices, shards(): lax.all_to_all(sent_moment, 'fsdp', split_axis=0, concat_axis=0, tiled=True)  89.4 us
    all_to_all x1, waiting for transfers between devices, shards(): lax.all_to_all(back_rows, 'fsdp', split_axis=0, concat_axis=0, tiled=True)  88.3 us
    all_to_all x1, starting transfers between devices, shards(): lax.all_to_all(sent_grad, 'fsdp', split_axis=0, concat_axis=0, tiled=True)  13.3 us
    all_to_all x1, starting transfers between devices, shards(): lax.all_to_all(sent_moment, 'fsdp', split_axis=0, concat_axis=0, tiled=True)  9.7 us
  transfers between devices with their start and end apart: 3, of which 2 were waited for; matrix products, arithmetic and copies ran while one was open for 5% of the time, Pallas kernels for 0%

commit v1 on v0

v1 whole, which is shorter than its diff:
```python
import functools

import jax
import jax.numpy as jnp
from jax import lax
from jax.experimental import pallas as pl
from jax.experimental.pallas import tpu as pltpu
from jax.sharding import PartitionSpec as P

CLIP_RMS = 0.5
FIRST_DECAY = 0.9
GRAM_DECAY = 0.95
GRAM_RATE = 0.05
SECOND_DECAY = 0.95
SECOND_RATE = 0.05
EPSILON = 1e-08

MESH = pl.DeviceIdType.MESH
NX, NZ, NC = 4, 8, 2
HALF = NZ // 2
COLBLK = 7
SLOTS = NX * NC
LOCAL = NX * COLBLK
ROWS = 64
BLOCK = 512
LANE = BLOCK // NX
CHUNKS = 2
RC = ROWS // CHUNKS
Z_ORDER = (4, 5, 3, 6, 2, 7, 1)
X_ORDER = (2, 1, 3)

BF16, F32 = jnp.bfloat16, jnp.float32


def mm(a, b):
    return jnp.dot(a, b, preferred_element_type=F32)


def kernel(
    n_entries,
    tgt_hbm,
    grad_hbm,
    first_hbm,
    lg_hbm,
    rg_hbm,
    ql_hbm,
    qr_hbm,
    sm_hbm,
    upd_hbm,
    fn_hbm,
    ln_hbm,
    rn_hbm,
    sn_hbm,
    g_v,
    f_v,
    lg_v,
    rg_v,
    ql_v,
    qr_v,
    sm_v,
    out_v,
    qlt_v,
    qrt_v,
    den_v,
    norm_s,
    norm_z,
    norm_x,
    norm_y,
    xs,
    xr,
    zs,
    zr_,
    gs,
    gr,
    blk,
    ub,
    ug,
    uz,
    us,
    uf,
    tgt_s,
    tgt_v,
    tbl_v,
    tbl,
    in_sem,
    out_sem,
    nsend,
    nrecv,
    xsend,
    xrecv,
    zsend,
    zrecv,
    gsend,
    grecv,
):
    f = lax.axis_index("fsdp")
    q = lax.axis_index("mp")
    tgt_loads = [
        pltpu.make_async_copy(tgt_hbm, tgt_s, in_sem.at[7]),
        pltpu.make_async_copy(tgt_hbm, tgt_v, in_sem.at[8]),
    ]
    for load in tgt_loads:
        load.start()
    c = lax.rem(f, NC)
    z = lax.rem(f // NC, NZ)
    x = f // (NC * NZ)
    n_mp = lax.axis_size("mp")

    def fid(xx, zz, cc):
        return (xx * NZ + zz) * NC + cc

    def rot(v, d, n):
        return lax.rem(v + d, n)

    loads = [
        pltpu.make_async_copy(src, dst, in_sem.at[i])
        for i, (src, dst) in enumerate(
            (
                (grad_hbm, g_v),
                (first_hbm, f_v),
                (ql_hbm, ql_v),
                (qr_hbm, qr_v),
                (sm_hbm, sm_v),
                (lg_hbm, lg_v),
                (rg_hbm, rg_v),
            )
        )
    ]
    for load in loads:
        load.start()

    barrier = pltpu.get_barrier_semaphore()
    peers = [(fid(x, rot(z, d, NZ), c), q) for d in Z_ORDER]
    peers += [
        (fid(rot(x, dx, NX), z, rot(c, dc, NC)), q)
        for dx in range(NX)
        for dc in range(NC)
        if dx or dc
    ]
    peers += [(f, rot(q, d, n_mp)) for d in range(1, n_mp)]
    for pf, pq in peers:
        pl.semaphore_signal(barrier, inc=1, device_id=(pf, pq), device_id_type=MESH)
    pl.semaphore_wait(barrier, len(peers))

    def send(src, dst, ssem, rsem, pf, pq):
        pltpu.make_async_remote_copy(
            src_ref=src,
            dst_ref=dst,
            send_sem=ssem,
            recv_sem=rsem,
            device_id=(pf, pq),
            device_id_type=MESH,
        ).start()

    def wait_bytes(ref, sem):
        pltpu.make_async_copy(ref, ref, sem).wait()

    def spread_stage(a, r, rows):
        for xx in range(NX):
            for j in range(COLBLK):
                lo = j * BLOCK + xx * LANE
                xs[a, r, xx, j] = rows[:, lo : lo + LANE]

    def spread_send(a, r):
        for d in X_ORDER:
            px = rot(x, d, NX)
            send(
                xs.at[a, r, px], xr[a][r].at[x], xsend.at[a, r], xrecv.at[a, r], fid(px, z, c), q
            )
        xr[a][r][x] = xs[a, r, x]

    def z_stage(a, r):
        wait_bytes(xr[a][r].at[pl.ds(0, NX - 1)], xrecv.at[a, r])

        def slots(pz, dst):
            for s in range(SLOTS):
                owner = fid(s // NC, pz, s % NC)
                l = tbl[0, owner]
                dst[s] = xr[a][r][l // COLBLK, lax.rem(l, COLBLK)]

        for d in Z_ORDER:
            pz = rot(z, d, NZ)
            slots(pz, zs.at[a, r, pz])
            send(
                zs.at[a, r, pz], zr_[a][r].at[z], zsend.at[a, r], zrecv.at[a, r], fid(x, pz, c), q
            )
        slots(z, zr_[a][r].at[z])

    def gather_stage(a, r):
        wait_bytes(zr_[a][r].at[pl.ds(0, NZ - 1)], zrecv.at[a, r])
        for s in range(SLOTS):
            h = tbl[1, fid(s // NC, z, s % NC)]
            for i in range(HALF):
                gs[a, r, s, i] = zr_[a][r][h * HALF + i, s]
        for dx in X_ORDER + (0,):
            for dc in range(NC):
                if dx or dc:
                    px, pc = rot(x, dx, NX), rot(c, dc, NC)
                    send(
                        gs.at[a, r, px * NC + pc],
                        gr.at[a, r, x, c],
                        gsend.at[a, r],
                        grecv.at[a, r],
                        fid(px, z, pc),
                        q,
                    )
        gr[a, r, x, c] = gs[a, r, x * NC + c]

    def assemble(a, r):
        wait_bytes(gs.at[a, r, pl.ds(0, SLOTS - 1)], grecv.at[a, r])
        for xx in range(NX):
            for cc in range(NC):
                for i in range(HALF):
                    blk[a, i * NC + cc, r * RC : (r + 1) * RC, xx * LANE : (xx + 1) * LANE] = gr[
                        a, r, xx, cc, i
                    ]

    loads[0].wait()
    for r in range(CHUNKS):
        spread_stage(0, r, g_v[r * RC : (r + 1) * RC, :])
        spread_send(0, r)

    for load in tgt_loads:
        load.wait()
    n_blocks = tgt_v.shape[1]
    sub = lax.broadcasted_iota(jnp.int32, (n_blocks, 128), 0)
    lane = lax.broadcasted_iota(jnp.int32, (n_blocks, 128), 1)
    sub_sq = lax.broadcasted_iota(jnp.int32, (n_blocks, n_blocks), 0)
    lane_sq = lax.broadcasted_iota(jnp.int32, (n_blocks, n_blocks), 1)
    diag = jnp.where(sub_sq == lane_sq, jnp.broadcast_to(tgt_v[...], sub_sq.shape), 0)
    named = jnp.sum(diag, axis=1, keepdims=True) == lane
    band = sub // COLBLK
    side = lax.rem(band, 2)
    local = jnp.where(side == z // HALF, sub - (band - band // 2) * COLBLK, 0)
    for i, code in enumerate((local, side, jnp.ones_like(sub))):
        tbl_v[i : i + 1, :] = jnp.max(jnp.where(named, code, 0), axis=0, keepdims=True)
    tbl_copy = pltpu.make_async_copy(tbl_v, tbl, in_sem.at[9])
    tbl_copy.start()

    wide = g_v[...].astype(F32)
    cols = jnp.sum((wide * wide).reshape(ROWS // 8, 8, wide.shape[1]), axis=0)
    acc = cols[:, :128]
    for i in range(1, cols.shape[1] // 128):
        acc = acc + cols[:, i * 128 : (i + 1) * 128]
    norm_s[0] = acc
    norm_z[z] = acc
    for d in Z_ORDER:
        send(norm_s.at[0], norm_z.at[z], nsend.at[0], nrecv.at[0], fid(x, rot(z, d, NZ), c), q)

    tbl_copy.wait()
    z_stage(0, 0)

    wait_bytes(norm_z.at[pl.ds(0, NZ - 1)], nrecv.at[0])
    acc = jnp.sum(norm_z[...], axis=0)
    norm_s[1] = acc
    norm_x[x] = acc
    for d in X_ORDER:
        send(norm_s.at[1], norm_x.at[x], nsend.at[1], nrecv.at[1], fid(rot(x, d, NX), z, c), q)

    for r in range(1, CHUNKS):
        z_stage(0, r)

    wait_bytes(norm_x.at[pl.ds(0, NX - 1)], nrecv.at[1])
    acc = jnp.sum(norm_x[...], axis=0)
    norm_s[2] = acc
    norm_y[q] = acc
    for d in range(1, n_mp):
        send(norm_s.at[2], norm_y.at[q], nsend.at[2], nrecv.at[2], f, rot(q, d, n_mp))
    wait_bytes(norm_y.at[pl.ds(0, n_mp - 1)], nrecv.at[2])
    acc = jnp.sum(norm_y[...], axis=0)
    norm_s[3] = acc
    norm_s[4] = acc
    send(norm_s.at[3], norm_s.at[5], nsend.at[3], nrecv.at[3], fid(x, z, 1 - c), q)
    wait_bytes(norm_s.at[5], nrecv.at[3])
    acc = norm_s[4] + norm_s[5]
    norm_sum = jnp.sum(jnp.sum(acc, axis=0, keepdims=True), axis=1, keepdims=True)
    clip = jnp.minimum(1.0, CLIP_RMS * (float(n_entries) ** 0.5) / jnp.sqrt(norm_sum))

    loads[1].wait()
    for r in range(CHUNKS):
        rows = slice(r * RC, (r + 1) * RC)
        nxt = FIRST_DECAY * f_v[rows, :] + ((1.0 - FIRST_DECAY) * clip) * g_v[rows, :].astype(F32)
        f_v[rows, :] = nxt
        spread_stage(1, r, nxt.astype(BF16))
        spread_send(1, r)
    stores = [pltpu.make_async_copy(f_v, fn_hbm, out_sem.at[0])]
    stores[0].start()
    for r in range(CHUNKS):
        z_stage(1, r)

    for load in loads[2:]:
        load.wait()
    left = ql_v[...].reshape(BLOCK, BLOCK)
    qlt_v[...] = left.T
    qrt_v[...] = qr_v[...].T
    for r in range(CHUNKS):
        gather_stage(0, r)
    for r in range(CHUNKS):
        assemble(0, r)
    live = tbl[2, f] > 0
    block = blk[0].reshape(BLOCK, BLOCK)
    half = mm(qlt_v[...], block).astype(BF16)
    rotated = clip * mm(half, qr_v[...])
    second = SECOND_DECAY * sm_v[...] + SECOND_RATE * rotated * rotated
    den_v[...] = jnp.sqrt(second) + EPSILON
    sm_v[...] = jnp.where(live, second, sm_v[...])
    stores.append(pltpu.make_async_copy(sm_v, sn_hbm, out_sem.at[1]))
    stores[-1].start()
    scale = GRAM_RATE * clip * clip / BLOCK
    block_t = block.T
    lg_v[...] = jnp.where(live, GRAM_DECAY * lg_v[...] + scale * mm(block, block_t), lg_v[...])
    stores.append(pltpu.make_async_copy(lg_v, ln_hbm, out_sem.at[2]))
    stores[-1].start()
    rg_v[...] = jnp.where(live, GRAM_DECAY * rg_v[...] + scale * mm(block_t, block), rg_v[...])
    stores.append(pltpu.make_async_copy(rg_v, rn_hbm, out_sem.at[3]))
    stores[-1].start()

    for r in range(CHUNKS):
        gather_stage(1, r)
    for r in range(CHUNKS):
        assemble(1, r)
    mhalf = mm(qlt_v[...], blk[1].reshape(BLOCK, BLOCK)).astype(BF16)
    normed = (mm(mhalf, qr_v[...]) / den_v[...]).astype(BF16)
    me = x * NC + c
    for r in range(CHUNKS):
        rows = ql_v[:, r * RC : (r + 1) * RC, :].reshape(HALF * NC * RC, BLOCK)
        upd = mm(mm(rows, normed).astype(BF16), qrt_v[...]).astype(BF16)
        for xx in range(NX):
            for cc in range(NC):
                for i in range(HALF):
                    lo = (i * NC + cc) * RC
                    ub[r, xx, cc, i] = upd[lo : lo + RC, xx * LANE : (xx + 1) * LANE]
        for dx in X_ORDER + (0,):
            for dc in range(NC):
                if dx or dc:
                    px, pc = rot(x, dx, NX), rot(c, dc, NC)
                    send(
                        ub.at[r, px, pc],
                        ug.at[r, me],
                        gsend.at[2, r],
                        grecv.at[2, r],
                        fid(px, z, pc),
                        q,
                    )
        ug[r, me] = ub[r, x, c]

    for r in range(CHUNKS):
        wait_bytes(ug.at[r, pl.ds(0, SLOTS - 1)], grecv.at[2, r])
        for d in Z_ORDER:
            pz = rot(z, d, NZ)
            send(
                ug.at[r, :, lax.rem(pz, HALF)],
                uz[r].at[z],
                zsend.at[2, r],
                zrecv.at[2, r],
                fid(x, pz, c),
                q,
            )
        for s in range(SLOTS):
            uz[r][z, s] = ug[r, s, lax.rem(z, HALF)]
    for r in range(CHUNKS):
        wait_bytes(uz[r].at[pl.ds(0, NZ - 1)], zrecv.at[2, r])
        for xx in range(NX):
            for j in range(COLBLK):
                t = tgt_s[0, (xx * 2 + z // HALF) * COLBLK + j]
                slot = (t // (NC * NZ)) * NC + lax.rem(t, NC)
                us[r, xx, j] = uz[r][lax.rem(t // NC, NZ), slot]
        for d in X_ORDER:
            px = rot(x, d, NX)
            send(us.at[r, px], uf.at[r, x], xsend.at[2, r], xrecv.at[2, r], fid(px, z, c), q)
        uf[r, x] = us[r, x]
    for r in range(CHUNKS):
        wait_bytes(uf.at[r, pl.ds(0, NX - 1)], xrecv.at[2, r])
        for xx in range(NX):
            for j in range(COLBLK):
                lo = j * BLOCK + xx * LANE
                out_v[r * RC : (r + 1) * RC, lo : lo + LANE] = uf[r, xx, j]
    stores.append(pltpu.make_async_copy(out_v, upd_hbm, out_sem.at[4]))
    stores[-1].start()

    wait_bytes(norm_z.at[pl.ds(0, NZ - 1)], nsend.at[0])
    wait_bytes(norm_x.at[pl.ds(0, NX - 1)], nsend.at[1])
    wait_bytes(norm_y.at[pl.ds(0, n_mp - 1)], nsend.at[2])
    wait_bytes(norm_s.at[3], nsend.at[3])
    for r in range(CHUNKS):
        for a in range(2):
            wait_bytes(xs.at[a, r, pl.ds(0, NX - 1)], xsend.at[a, r])
            wait_bytes(zs.at[a, r, pl.ds(0, NZ - 1)], zsend.at[a, r])
            wait_bytes(gs.at[a, r, pl.ds(0, SLOTS - 1)], gsend.at[a, r])
        wait_bytes(ug.at[r, pl.ds(0, SLOTS - 1)], gsend.at[2, r])
        wait_bytes(uz[r].at[pl.ds(0, NZ - 1)], zsend.at[2, r])
        wait_bytes(us.at[r, pl.ds(0, NX - 1)], xsend.at[2, r])
    for store in stores:
        store.wait()


def shards(
    gradient,
    first_moment,
    left_gram,
    right_gram,
    left_basis,
    right_basis,
    second_moment,
    block_target,
):
    rows, cols = gradient.shape
    n_fsdp = lax.axis_size("fsdp")
    n_mp = lax.axis_size("mp")
    n_blocks = block_target.shape[1]
    any_spec = pl.BlockSpec(memory_space=pl.ANY)
    vm = pltpu.VMEM
    dma = pltpu.SemaphoreType.DMA
    mat = (BLOCK, BLOCK)
    out = pl.pallas_call(
        functools.partial(kernel, rows * cols * n_fsdp * n_mp),
        out_shape=(
            jax.ShapeDtypeStruct((rows, cols), BF16),
            jax.ShapeDtypeStruct((rows, cols), F32),
            jax.ShapeDtypeStruct(mat, F32),
            jax.ShapeDtypeStruct(mat, F32),
            jax.ShapeDtypeStruct(mat, F32),
        ),
        in_specs=[any_spec] * 8,
        out_specs=(any_spec,) * 5,
        scratch_shapes=[
            vm((rows, cols), BF16),
            vm((rows, cols), F32),
            vm(mat, F32),
            vm(mat, F32),
            vm((HALF * NC, ROWS, BLOCK), BF16),
            vm(mat, BF16),
            vm(mat, F32),
            vm((rows, cols), BF16),
            vm(mat, BF16),
            vm(mat, BF16),
            vm(mat, F32),
            vm((6, 8, 128), F32),
            vm((NZ, 8, 128), F32),
            vm((NX, 8, 128), F32),
            vm((n_mp, 8, 128), F32),
            vm((2, CHUNKS, NX, COLBLK, RC, LANE), BF16),
            [[vm((NX, COLBLK, RC, LANE), BF16)] * CHUNKS] * 2,
            vm((2, CHUNKS, NZ, SLOTS, RC, LANE), BF16),
            [[vm((NZ, SLOTS, RC, LANE), BF16)] * CHUNKS] * 2,
            vm((2, CHUNKS, SLOTS, HALF, RC, LANE), BF16),
            vm((2, CHUNKS, NX, NC, HALF, RC, LANE), BF16),
            vm((2, HALF * NC, ROWS, BLOCK), BF16),
            vm((CHUNKS, NX, NC, HALF, RC, LANE), BF16),
            vm((CHUNKS, SLOTS, HALF, RC, LANE), BF16),
            [vm((NZ, SLOTS, RC, LANE), BF16)] * CHUNKS,
            vm((CHUNKS, NX, COLBLK, RC, LANE), BF16),
            vm((CHUNKS, NX, COLBLK, RC, LANE), BF16),
            pltpu.SMEM((1, n_blocks), jnp.int32),
            vm((1, n_blocks), jnp.int32),
            vm((8, 128), jnp.int32),
            pltpu.SMEM((8, 128), jnp.int32),
            dma((10,)),
            dma((5,)),
            dma((4,)),
            dma((4,)),
            dma((3, CHUNKS)),
            dma((3, CHUNKS)),
            dma((3, CHUNKS)),
            dma((3, CHUNKS)),
            dma((3, CHUNKS)),
            dma((3, CHUNKS)),
        ],
        compiler_params=pltpu.CompilerParams(
            collective_id=0, has_side_effects=True, vmem_limit_bytes=60 * 2**20
        ),
        cost_estimate=pl.CostEstimate(
            flops=16 * BLOCK**3, bytes_accessed=12 * 2**20, transcendentals=BLOCK**2
        ),
    )(
        block_target,
        gradient,
        first_moment,
        left_gram[0, 0],
        right_gram[0, 0],
        left_basis[0, 0].reshape(HALF * NC, ROWS, BLOCK),
        right_basis[0, 0],
        second_moment[0, 0],
    )
    return (out[0], out[1]) + tuple(o[None, None] for o in out[2:])


def solution(mesh):
    return jax.shard_map(
        shards,
        mesh=mesh,
        in_specs=(
            P("fsdp", "mp"),
            P("fsdp", "mp"),
            P("fsdp", "mp", None, None),
            P("fsdp", "mp", None, None),
            P("fsdp", "mp", None, None),
            P("fsdp", "mp", None, None),
            P("fsdp", "mp", None, None),
            P("mp", None),
        ),
        out_specs=(
            P("fsdp", "mp"),
            P("fsdp", "mp"),
            P("fsdp", "mp", None, None),
            P("fsdp", "mp", None, None),
            P("fsdp", "mp", None, None),
        ),
        check_vma=False,
    )
```

time: 393 us -> 111 us (0.28)
  waiting for transfers between devices: 178 us -> 0 us
  blocking collectives: 137 us -> 0 us
  Pallas kernels: 0 us -> 102 us
  starting transfers between devices: 29.1 us -> 0 us
  matrix products: 19.6 us -> 0 us
  other arithmetic: 11 us -> 0 us
  local copies, waits for them, and re-layouts: 15.7 us -> 7.63 us
    all_to_all x3 -> x0, waiting for transfers between devices: 178 us -> none  [the longest x1 89.4 us: shards(): lax.all_to_all(sent_moment, 'fsdp', split_axis=0, concat_axis=0, tiled=True)]
    psum x1 -> x0, blocking collectives: 137 us -> none  [shards(): norm_sum = lax.psum(jnp.sum(grad_wide * grad_wide), ('fsdp', 'mp'))]
    pallas_call x0 -> x1, Pallas kernels: none -> 102 us  [shards(): pl.pallas_call(functools.partial(kernel, rows * cols * n_fsdp * n_mp), ou...]
    all_to_all x3 -> x0, starting transfers between devices: 29.1 us -> none  [the longest x1 13.3 us: shards(): lax.all_to_all(sent_grad, 'fsdp', split_axis=0, concat_axis=0, tiled=True)]
    dot_general x8 -> x0, matrix products: 19.6 us -> none  [the longest x1 4.51 us: shards(): jnp.einsum('jo,orc->rjc', to_owner, came_back, preferred_element_type=jnp...]
    convert_element_type x2 -> x0, local copies, waits for them, and re-layouts: 8.71 us -> none  [the longest x1 4.37 us: shards(): sent_moment = jnp.einsum('jo,rjc->orc', to_owner, moment_pieces, preferre...]
    unnamed x17 -> x13, local copies, waits for them, and re-layouts: 0.98 us -> 7.63 us
  transfers between devices with their start and end apart: 3 -> 0, of which waited for: 2 -> 0; matrix products, arithmetic and copies ran while one was open for 5% -> 0% of each run, Pallas kernels for 0% -> 0%
where the time goes in v1:
time: 111 us; the launch traced here: 110 us
  Pallas kernels  102 us (92%)
  local copies, waits for them, and re-layouts  7.63 us (7%)
    pallas_call x1, Pallas kernels, shards(): pl.pallas_call(functools.partial(kernel, rows * cols * n_fsdp * n_mp), ou...  102 us
    unnamed x13, local copies, waits for them, and re-layouts  7.63 us

profile of v1, /device:TPU:1, one launch (start us, length us, event | category | flops | bytes accessed | tf_op | source)
XLA Modules:
  0.0 110.4 jit_solution(10667946346084173618)
XLA Ops:
  0.6 102.1 %shard_map.119 = (bf16[64,3584]{1,0:T(8,128)(2,1)}, f32[64,3584]{1,0:T(8,128)}, f32[512,512]{1,0:T(8,128)}, f32[512,512]{1,0:T(8,128)}, f32[512,512]{1,0:T(8,128)}) custom-call(s32[1,56]{1,0:T(1,128)} %tgt_hbm.1, bf16[64,3584]{1,0:T(8,128)(2,1)} %grad_hbm.1, f32[64,3584]{1,0:T(8,128)} %first_hbm.1, f32[512,512]{1,0:T(8,128)} %bitcast.11, ...), custom_call_target="tpu_custom_call" | custom-call | flops 2147483648 | bytes 12582912 | tf_op jit(solution)/shard_map/pallas_call | solution.py:415
  102.8 0.0 copy-start.3
  102.8 1.9 %copy.18 = bf16[64,3584]{1,0:T(8,128)(2,1)} copy(bf16[64,3584]{1,0:T(8,128)(2,1)} %get-tuple-element.20) | data formatting | bytes 917504
  104.7 0.0 copy-done.3
  104.7 0.0 copy-start.2
  104.7 0.9 copy.19
  105.6 0.6 copy-done.2
  106.2 0.0 copy-start.1
  106.2 1.0 copy.20
  107.2 0.6 copy-done.1
  107.8 0.0 copy-start
  107.8 1.0 copy.21
  108.8 0.6 copy-done
  109.4 1.0 copy.22
Async XLA Ops:
  102.8 1.9 %copy-start.3 = (f32[64,3584]{1,0:T(8,128)S(1)}, f32[64,3584]{1,0:T(8,128)}, u32[]{:S(2)}) copy-start(f32[64,3584]{1,0:T(8,128)} %get-tuple-element.21) | copy-start | bytes 2752516
  104.7 1.6 %copy-start.2 = (f32[512,512]{1,0:T(8,128)S(1)}, f32[512,512]{1,0:T(8,128)}, u32[]{:S(2)}) copy-start(f32[512,512]{1,0:T(8,128)} %get-tuple-element.12) | copy-start | bytes 3145732
  106.2 1.6 %copy-start.1 = (f32[512,512]{1,0:T(8,128)S(1)}, f32[512,512]{1,0:T(8,128)}, u32[]{:S(2)}) copy-start(f32[512,512]{1,0:T(8,128)} %get-tuple-element.13) | copy-start | bytes 3145732
  107.8 1.6 %copy-start = (f32[512,512]{1,0:T(8,128)S(1)}, f32[512,512]{1,0:T(8,128)}, u32[]{:S(2)}) copy-start(f32[512,512]{1,0:T(8,128)} %get-tuple-element.14) | copy-start | bytes 3145732

commit v2 on v1

v2 whole, which is shorter than its diff:
```python
import functools

import jax
import jax.numpy as jnp
from jax import lax
from jax.experimental import pallas as pl
from jax.experimental.pallas import tpu as pltpu
from jax.sharding import PartitionSpec as P

CLIP_RMS = 0.5
FIRST_DECAY = 0.9
GRAM_DECAY = 0.95
GRAM_RATE = 0.05
SECOND_DECAY = 0.95
SECOND_RATE = 0.05
EPSILON = 1e-08

MESH = pl.DeviceIdType.MESH
NX, NZ, NC = 4, 8, 2
HALF = NZ // 2
COLBLK = 7
SLOTS = NX * NC
LOCAL = NX * COLBLK
ROWS = 64
BLOCK = 512
LANE = BLOCK // NX
CHUNKS = 4
DIRECT = 2
RC = ROWS // CHUNKS
Z_ORDER = (4, 5, 3, 6, 2, 7, 1)
X_ORDER = (2, 1, 3)

BF16, F32 = jnp.bfloat16, jnp.float32


def mm(a, b):
    return jnp.dot(a, b, preferred_element_type=F32)


def kernel(
    n_entries,
    tgt_hbm,
    grad_hbm,
    first_hbm,
    lg_hbm,
    rg_hbm,
    ql_hbm,
    qr_hbm,
    sm_hbm,
    out_v,
    f_v,
    lg_v,
    rg_v,
    sm_v,
    g_v,
    ql_v,
    qr_v,
    qlt_v,
    qrt_v,
    den_v,
    norm_s,
    norm_y,
    norm_x,
    norm_z,
    xs,
    xr,
    zs,
    zr,
    gs,
    gr,
    blk,
    ms,
    mx,
    mzs,
    mz,
    uds,
    udz,
    udp,
    udx,
    ub,
    ug,
    uz,
    us,
    uf,
    tgt_s,
    tgt_v,
    tbl_v,
    tbl,
    in_sem,
    nsend,
    nrecv,
    xsend,
    xrecv,
    zsend,
    zrecv,
    gsend,
    grecv,
):
    f = lax.axis_index("fsdp")
    q = lax.axis_index("mp")
    c = lax.rem(f, NC)
    z = lax.rem(f // NC, NZ)
    x = f // (NC * NZ)
    side_here = z // HALF
    n_mp = lax.axis_size("mp")

    def fid(xx, zz, cc):
        return (xx * NZ + zz) * NC + cc

    def rot(v, d, n):
        return lax.rem(v + d, n)

    tgt_loads = [
        pltpu.make_async_copy(tgt_hbm, tgt_s, in_sem.at[7]),
        pltpu.make_async_copy(tgt_hbm, tgt_v, in_sem.at[8]),
    ]
    loads = [
        pltpu.make_async_copy(src, dst, in_sem.at[i])
        for i, (src, dst) in enumerate(
            (
                (grad_hbm, g_v),
                (first_hbm, f_v),
                (ql_hbm, ql_v),
                (qr_hbm, qr_v),
                (sm_hbm, sm_v),
                (lg_hbm, lg_v),
                (rg_hbm, rg_v),
            )
        )
    ]
    for load in loads[:1] + tgt_loads + loads[1:]:
        load.start()

    near = [(dx, dc) for dx in X_ORDER + (0,) for dc in range(NC) if dx or dc]
    barrier = pltpu.get_barrier_semaphore()
    peers = [(fid(x, rot(z, d, NZ), rot(c, dc, NC)), q) for d in Z_ORDER for dc in range(NC)]
    peers += [(fid(rot(x, dx, NX), z, rot(c, dc, NC)), q) for dx, dc in near]
    peers += [(f, rot(q, d, n_mp)) for d in range(1, n_mp)]
    for peer in peers:
        pl.semaphore_signal(barrier, inc=1, device_id=peer, device_id_type=MESH)

    for load in tgt_loads:
        load.wait()
    n_blocks = tgt_v.shape[1]
    sub = lax.broadcasted_iota(jnp.int32, (n_blocks, 128), 0)
    lane = lax.broadcasted_iota(jnp.int32, (n_blocks, 128), 1)
    sub_sq = lax.broadcasted_iota(jnp.int32, (n_blocks, n_blocks), 0)
    lane_sq = lax.broadcasted_iota(jnp.int32, (n_blocks, n_blocks), 1)
    diag = jnp.where(sub_sq == lane_sq, jnp.broadcast_to(tgt_v[...], sub_sq.shape), 0)
    named = jnp.sum(diag, axis=1, keepdims=True) == lane
    band = sub // COLBLK
    side = lax.rem(band, 2)
    local = jnp.where(side == side_here, sub - (band - band // 2) * COLBLK, 0)
    for i, code in enumerate((local, side, jnp.ones_like(sub))):
        tbl_v[i : i + 1, :] = jnp.max(jnp.where(named, code, 0), axis=0, keepdims=True)
    tbl_copy = pltpu.make_async_copy(tbl_v, tbl, in_sem.at[9])
    tbl_copy.start()

    with jax.named_scope("barrier"):
        pl.semaphore_wait(barrier, len(peers))

    def send(src, dst, ssem, rsem, pf, pq=q):
        pltpu.make_async_remote_copy(
            src_ref=src,
            dst_ref=dst,
            send_sem=ssem,
            recv_sem=rsem,
            device_id=(pf, pq),
            device_id_type=MESH,
        ).start()

    def wait_bytes(ref, sem):
        pltpu.make_async_copy(ref, ref, sem).wait()

    def some(ref, n):
        return ref.at[pl.ds(0, n)]

    def all_but_one(ref):
        return some(ref, ref.shape[0] - 1)

    def g_spread(r):
        rows = g_v[r * RC : (r + 1) * RC, :]
        for xx in range(NX):
            for j in range(COLBLK):
                lo = j * BLOCK + xx * LANE
                xs[r, xx, j] = rows[:, lo : lo + LANE]
        for d in X_ORDER:
            px = rot(x, d, NX)
            send(xs.at[r, px], xr[r].at[x], xsend.at[0, r], xrecv.at[0, r], fid(px, z, c))
        xr[r][x] = xs[r, x]

    def g_exchange(r):
        with jax.named_scope("g_spread_wait"):
            wait_bytes(all_but_one(xr[r]), xrecv.at[0, r])

        def slots(pz, dst):
            for s in range(SLOTS):
                l = tbl[0, fid(s // NC, pz, s % NC)]
                dst[s] = xr[r][l // COLBLK, lax.rem(l, COLBLK)]

        for d in Z_ORDER:
            pz = rot(z, d, NZ)
            slots(pz, zs.at[r, pz])
            send(zs.at[r, pz], zr[r].at[z], zsend.at[0, r], zrecv.at[0, r], fid(x, pz, c))
        slots(z, zr[r].at[z])

    def g_gather(r):
        with jax.named_scope("g_exchange_wait"):
            wait_bytes(all_but_one(zr[r]), zrecv.at[0, r])
        for s in range(SLOTS):
            h = tbl[1, fid(s // NC, z, s % NC)]
            for i in range(HALF):
                gs[r, s, i] = zr[r][h * HALF + i, s]
        for dx, dc in near:
            px, pc = rot(x, dx, NX), rot(c, dc, NC)
            send(
                gs.at[r, px * NC + pc],
                gr.at[r, x, c],
                gsend.at[0, r],
                grecv.at[0, r],
                fid(px, z, pc),
            )
        gr[r, x, c] = gs[r, x * NC + c]

    def g_assemble(r):
        with jax.named_scope("g_gather_wait"):
            wait_bytes(all_but_one(gs.at[r]), grecv.at[0, r])
        for xx in range(NX):
            for cc in range(NC):
                for i in range(HALF):
                    blk[0, i * NC + cc, r * RC : (r + 1) * RC, xx * LANE : (xx + 1) * LANE] = gr[
                        r, xx, cc, i
                    ]

    def m_spread(r):
        for d in X_ORDER:
            send(ms.at[r], mx[r].at[x], xsend.at[1, r], xrecv.at[1, r], fid(rot(x, d, NX), z, c))
        mx[r][x] = ms[r]

    def m_exchange(r):
        with jax.named_scope("m_spread_wait"):
            wait_bytes(all_but_one(mx[r]), xrecv.at[1, r])

        def slot(pz, pc, dst):
            l = tbl[0, fid(x, pz, pc)]
            dst[...] = mx[r][l // COLBLK, lax.rem(l, COLBLK)]

        for d in Z_ORDER + (0,):
            pz = rot(z, d, NZ)
            for dc in range(NC):
                pc = rot(c, dc, NC)
                if d or dc:
                    slot(pz, pc, mzs.at[r, pz * NC + pc])
                    send(
                        mzs.at[r, pz * NC + pc],
                        mz[r].at[z * NC + c],
                        zsend.at[1, r],
                        zrecv.at[1, r],
                        fid(x, pz, pc),
                    )
        slot(z, c, mz[r].at[z * NC + c])


    def m_assemble(r):
        with jax.named_scope("m_exchange_wait"):
            wait_bytes(all_but_one(mz[r]), zrecv.at[1, r])
        h = tbl[1, f]
        for i in range(HALF):
            for cc in range(NC):
                blk[1, i * NC + cc, r * RC : (r + 1) * RC, :] = mz[r][(h * HALF + i) * NC + cc]

    def d_exchange(r, upd):
        for i in range(HALF):
            for cc in range(NC):
                lo = (i * NC + cc) * RC
                uds[r, i, cc] = upd[lo : lo + RC, :]
        for d in Z_ORDER + (0,):
            pz = rot(z, d, NZ)
            for dc in range(NC):
                pc = rot(c, dc, NC)
                if d or dc:
                    send(
                        uds.at[r, lax.rem(pz, HALF), pc],
                        udz[r].at[z * NC + c],
                        zsend.at[2, r],
                        zrecv.at[2, r],
                        fid(x, pz, pc),
                    )
        udz[r][z * NC + c] = uds[r, lax.rem(z, HALF), c]

    def d_gather(r):
        with jax.named_scope("d_exchange_wait"):
            wait_bytes(all_but_one(udz[r]), zrecv.at[2, r])
        for d in X_ORDER + (0,):
            px = rot(x, d, NX)
            for j in range(COLBLK):
                t = tgt_s[0, (px * 2 + side_here) * COLBLK + j]
                part = udz[r][lax.rem(t, NZ * NC)]
                if d:
                    udp[r, px, j] = part
                else:
                    udx[r][x, j] = part
            if d:
                send(udp.at[r, px], udx[r].at[x], xsend.at[2, r], xrecv.at[2, r], fid(px, z, c))

    def d_finish(r):
        with jax.named_scope("d_gather_wait"):
            wait_bytes(all_but_one(udx[r]), xrecv.at[2, r])
        for j in range(COLBLK):
            t = tgt_s[0, (x * 2 + side_here) * COLBLK + j]
            out_v[r * RC : (r + 1) * RC, j * BLOCK : (j + 1) * BLOCK] = udx[r][t // (NZ * NC), j]

    me = x * NC + c

    def u_spread(r, upd):
        for xx in range(NX):
            for cc in range(NC):
                for i in range(HALF):
                    lo = (i * NC + cc) * RC
                    ub[r, xx, cc, i] = upd[lo : lo + RC, xx * LANE : (xx + 1) * LANE]
        for dx, dc in near:
            px, pc = rot(x, dx, NX), rot(c, dc, NC)
            send(ub.at[r, px, pc], ug.at[r, me], gsend.at[2, r], grecv.at[2, r], fid(px, z, pc))
        ug[r, me] = ub[r, x, c]

    def u_exchange(r):
        with jax.named_scope("u_spread_wait"):
            wait_bytes(all_but_one(ug.at[r]), grecv.at[2, r])
        for d in Z_ORDER:
            pz = rot(z, d, NZ)
            send(
                ug.at[r, :, lax.rem(pz, HALF)],
                uz[r].at[z],
                zsend.at[2, r],
                zrecv.at[2, r],
                fid(x, pz, c),
            )
        for s in range(SLOTS):
            uz[r][z, s] = ug[r, s, lax.rem(z, HALF)]

    def u_gather(r):
        with jax.named_scope("u_exchange_wait"):
            wait_bytes(all_but_one(uz[r]), zrecv.at[2, r])
        for d in X_ORDER + (0,):
            px = rot(x, d, NX)
            for j in range(COLBLK):
                t = tgt_s[0, (px * 2 + side_here) * COLBLK + j]
                slot = (t // (NC * NZ)) * NC + lax.rem(t, NC)
                part = uz[r][lax.rem(t // NC, NZ), slot]
                if d:
                    us[r, px, j] = part
                else:
                    uf[r, x, j] = part
            if d:
                send(us.at[r, px], uf.at[r, x], xsend.at[2, r], xrecv.at[2, r], fid(px, z, c))

    def u_finish(r):
        with jax.named_scope("u_gather_wait"):
            wait_bytes(all_but_one(uf.at[r]), xrecv.at[2, r])
        for xx in range(NX):
            for j in range(COLBLK):
                lo = j * BLOCK + xx * LANE
                out_v[r * RC : (r + 1) * RC, lo : lo + LANE] = uf[r, xx, j]

    loads[0].wait()
    g_spread(0)
    wide = g_v[...].astype(F32)
    cols = jnp.sum((wide * wide).reshape(ROWS // 8, 8, wide.shape[1]), axis=0)
    acc = cols[:, :128]
    for i in range(1, cols.shape[1] // 128):
        acc = acc + cols[:, i * 128 : (i + 1) * 128]
    norm_s[0] = acc
    norm_y[q] = acc
    for d in range(1, n_mp):
        send(norm_s.at[0], norm_y.at[q], nsend.at[0], nrecv.at[0], f, rot(q, d, n_mp))
    g_spread(1)
    tbl_copy.wait()
    g_exchange(0)
    g_spread(2)

    wait_bytes(all_but_one(norm_y), nrecv.at[0])
    acc = jnp.sum(norm_y[...], axis=0)
    norm_s[1] = acc
    norm_x[me] = acc
    for dx, dc in near:
        send(
            norm_s.at[1],
            norm_x.at[me],
            nsend.at[1],
            nrecv.at[1],
            fid(rot(x, dx, NX), z, rot(c, dc, NC)),
        )
    g_exchange(1)
    g_spread(3)
    with jax.named_scope("norm_x_wait"):
        wait_bytes(all_but_one(norm_x), nrecv.at[1])
    acc = jnp.sum(norm_x[...], axis=0)
    norm_s[2] = acc
    norm_z[z] = acc
    for d in Z_ORDER:
        send(norm_s.at[2], norm_z.at[z], nsend.at[2], nrecv.at[2], fid(x, rot(z, d, NZ), c))
    g_exchange(2)
    g_exchange(3)
    with jax.named_scope("norm_z_wait"):
        wait_bytes(all_but_one(norm_z), nrecv.at[2])
    acc = jnp.sum(norm_z[...], axis=0)
    norm_sum = jnp.sum(jnp.sum(acc, axis=0, keepdims=True), axis=1, keepdims=True)
    clip = jnp.minimum(1.0, CLIP_RMS * (float(n_entries) ** 0.5) / jnp.sqrt(norm_sum))

    loads[1].wait()
    for r in range(CHUNKS):
        rows = slice(r * RC, (r + 1) * RC)
        nxt = FIRST_DECAY * f_v[rows, :] + ((1.0 - FIRST_DECAY) * clip) * g_v[rows, :].astype(F32)
        f_v[rows, :] = nxt
        low = nxt.astype(BF16)
        for j in range(COLBLK):
            ms[r, j] = low[:, j * BLOCK : (j + 1) * BLOCK]
        if r < 2:
            m_spread(r)
    for load in loads[2:]:
        load.wait()
    qlt_v[...] = ql_v[...].reshape(BLOCK, BLOCK).T
    qrt_v[...] = qr_v[...].T
    g_gather(0)
    m_exchange(0)
    m_spread(2)
    g_gather(1)
    m_exchange(1)
    m_spread(3)
    g_gather(2)
    m_exchange(2)
    g_gather(3)
    m_exchange(3)

    for r in range(CHUNKS):
        g_assemble(r)
    with jax.named_scope("owner_gradient"):
        live = tbl[2, f] > 0
        block = blk[0].reshape(BLOCK, BLOCK)
        half = mm(qlt_v[...], block).astype(BF16)
        rotated = clip * mm(half, qr_v[...])
        second = SECOND_DECAY * sm_v[...] + SECOND_RATE * rotated * rotated
        den_v[...] = jnp.sqrt(second) + EPSILON
        sm_v[...] = jnp.where(live, second, sm_v[...])
        scale = GRAM_RATE * clip * clip / BLOCK
        block_t = block.T
        lg_v[...] = jnp.where(live, GRAM_DECAY * lg_v[...] + scale * mm(block, block_t), lg_v[...])
        rg_v[...] = jnp.where(live, GRAM_DECAY * rg_v[...] + scale * mm(block_t, block), rg_v[...])

    for r in range(CHUNKS):
        m_assemble(r)
    with jax.named_scope("owner_moment"):
        mhalf = mm(qlt_v[...], blk[1].reshape(BLOCK, BLOCK)).astype(BF16)
        normed = (mm(mhalf, qr_v[...]) / den_v[...]).astype(BF16)
    for r in range(CHUNKS):
        rows = ql_v[:, r * RC : (r + 1) * RC, :].reshape(HALF * NC * RC, BLOCK)
        upd = mm(mm(rows, normed).astype(BF16), qrt_v[...]).astype(BF16)
        if r < DIRECT:
            d_exchange(r, upd)
        else:
            u_spread(r, upd)
    for r in range(DIRECT, CHUNKS):
        u_exchange(r)
    for r in range(DIRECT):
        d_gather(r)
    for r in range(DIRECT, CHUNKS):
        u_gather(r)
    for r in range(DIRECT):
        d_finish(r)
    for r in range(DIRECT, CHUNKS):
        u_finish(r)

    wait_bytes(all_but_one(norm_y), nsend.at[0])
    wait_bytes(all_but_one(norm_x), nsend.at[1])
    wait_bytes(all_but_one(norm_z), nsend.at[2])
    for r in range(CHUNKS):
        wait_bytes(all_but_one(xr[r]), xsend.at[0, r])
        wait_bytes(all_but_one(zr[r]), zsend.at[0, r])
        wait_bytes(all_but_one(gs.at[r]), gsend.at[0, r])
        wait_bytes(all_but_one(mx[r]), xsend.at[1, r])
        wait_bytes(all_but_one(mz[r]), zsend.at[1, r])
        if r < DIRECT:
            wait_bytes(all_but_one(udz[r]), zsend.at[2, r])
            wait_bytes(all_but_one(udx[r]), xsend.at[2, r])
        else:
            wait_bytes(all_but_one(ug.at[r]), gsend.at[2, r])
            wait_bytes(all_but_one(uz[r]), zsend.at[2, r])
            wait_bytes(all_but_one(uf.at[r]), xsend.at[2, r])


def write_out(*refs):
    n = (len(refs) - 1) // 2
    copies = [
        pltpu.make_async_copy(refs[i], refs[n + i], refs[-1].at[i]) for i in range(n)
    ]
    for copy in copies:
        copy.start()
    for copy in copies:
        copy.wait()


def shards(
    gradient,
    first_moment,
    left_gram,
    right_gram,
    left_basis,
    right_basis,
    second_moment,
    block_target,
):
    rows, cols = gradient.shape
    n_fsdp = lax.axis_size("fsdp")
    n_mp = lax.axis_size("mp")
    n_blocks = block_target.shape[1]
    any_spec = pl.BlockSpec(memory_space=pl.ANY)
    vmem_spec = pl.BlockSpec(memory_space=pltpu.VMEM)
    vm = pltpu.VMEM
    dma = pltpu.SemaphoreType.DMA
    mat = (BLOCK, BLOCK)
    piece = (RC, LANE)
    strip = (RC, BLOCK)

    def per_chunk(n, *shape):
        return [vm(shape, BF16) for _ in range(n)]

    shapes = [((rows, cols), BF16), ((rows, cols), F32)] + [(mat, F32)] * 3
    held = pl.pallas_call(
        functools.partial(kernel, rows * cols * n_fsdp * n_mp),
        out_shape=tuple(vm(s, d) for s, d in shapes),
        in_specs=[any_spec] * 8,
        out_specs=(vmem_spec,) * 5,
        scratch_shapes=[
            vm((rows, cols), BF16),
            vm((HALF * NC, ROWS, BLOCK), BF16),
            vm(mat, BF16),
            vm(mat, BF16),
            vm(mat, BF16),
            vm(mat, F32),
            vm((3, 8, 128), F32),
            vm((n_mp, 8, 128), F32),
            vm((SLOTS, 8, 128), F32),
            vm((NZ, 8, 128), F32),
            vm((CHUNKS, NX, COLBLK) + piece, BF16),
            per_chunk(CHUNKS, NX, COLBLK, *piece),
            vm((CHUNKS, NZ, SLOTS) + piece, BF16),
            per_chunk(CHUNKS, NZ, SLOTS, *piece),
            vm((CHUNKS, SLOTS, HALF) + piece, BF16),
            vm((CHUNKS, NX, NC, HALF) + piece, BF16),
            vm((2, HALF * NC, ROWS, BLOCK), BF16),
            vm((CHUNKS, COLBLK) + strip, BF16),
            per_chunk(CHUNKS, NX, COLBLK, *strip),
            vm((CHUNKS, NZ * NC) + strip, BF16),
            per_chunk(CHUNKS, NZ * NC, *strip),
            vm((DIRECT, HALF, NC) + strip, BF16),
            per_chunk(DIRECT, NZ * NC, *strip),
            vm((DIRECT, NX, COLBLK) + strip, BF16),
            per_chunk(DIRECT, NX, COLBLK, *strip),
            vm((CHUNKS, NX, NC, HALF) + piece, BF16),
            vm((CHUNKS, SLOTS, HALF) + piece, BF16),
            per_chunk(CHUNKS, NZ, SLOTS, *piece),
            vm((CHUNKS, NX, COLBLK) + piece, BF16),
            vm((CHUNKS, NX, COLBLK) + piece, BF16),
            pltpu.SMEM((1, n_blocks), jnp.int32),
            vm((1, n_blocks), jnp.int32),
            vm((8, 128), jnp.int32),
            pltpu.SMEM((8, 128), jnp.int32),
            dma((10,)),
            dma((3,)),
            dma((3,)),
        ]
        + [dma((3, CHUNKS))] * 6,
        compiler_params=pltpu.CompilerParams(
            collective_id=0, has_side_effects=True, vmem_limit_bytes=59 * 2**20
        ),
        cost_estimate=pl.CostEstimate(
            flops=16 * BLOCK**3, bytes_accessed=12 * 2**20, transcendentals=BLOCK**2
        ),
    )(
        block_target,
        gradient,
        first_moment,
        left_gram[0, 0],
        right_gram[0, 0],
        left_basis[0, 0].reshape(HALF * NC, ROWS, BLOCK),
        right_basis[0, 0],
        second_moment[0, 0],
    )
    out = pl.pallas_call(
        write_out,
        out_shape=tuple(jax.ShapeDtypeStruct(s, d) for s, d in shapes),
        in_specs=[vmem_spec] * 5,
        out_specs=(any_spec,) * 5,
        scratch_shapes=[dma((5,))],
        compiler_params=pltpu.CompilerParams(vmem_limit_bytes=2**20),
    )(*held)
    return (out[0], out[1]) + tuple(o[None, None] for o in out[2:])


def solution(mesh):
    return jax.shard_map(
        shards,
        mesh=mesh,
        in_specs=(
            P("fsdp", "mp"),
            P("fsdp", "mp"),
            P("fsdp", "mp", None, None),
            P("fsdp", "mp", None, None),
            P("fsdp", "mp", None, None),
            P("fsdp", "mp", None, None),
            P("fsdp", "mp", None, None),
            P("mp", None),
        ),
        out_specs=(
            P("fsdp", "mp"),
            P("fsdp", "mp"),
            P("fsdp", "mp", None, None),
            P("fsdp", "mp", None, None),
            P("fsdp", "mp", None, None),
        ),
        check_vma=False,
    )
```

time: 111 us -> 93.2 us (0.84)
  Pallas kernels: 102 us -> 92.2 us
  local copies, waits for them, and re-layouts: 7.63 us -> 0 us
    pallas_call x1, Pallas kernels: 102 us -> 90 us  [shards(): pl.pallas_call(functools.partial(kernel, rows * cols * n_fsdp * n_mp), ou...]
    unnamed x13 -> x0, local copies, waits for them, and re-layouts: 7.63 us -> none
    pallas_call x0 -> x1, Pallas kernels: none -> 2.16 us  [shards(): pl.pallas_call(write_out, out_shape=tuple((jax.ShapeDtypeStruct(s, d) for...]
where the time goes in v2:
time: 93.2 us; the launch traced here: 92.8 us
  Pallas kernels  92.2 us (99%)
    pallas_call x1, Pallas kernels, shards(): pl.pallas_call(functools.partial(kernel, rows * cols * n_fsdp * n_mp), ou...  90 us
    pallas_call x1, Pallas kernels, shards(): pl.pallas_call(write_out, out_shape=tuple((jax.ShapeDtypeStruct(s, d) for...  2.16 us

profile of v2, /device:TPU:1, one launch (start us, length us, event | category | flops | bytes accessed | tf_op | source)
XLA Modules:
  0.0 92.8 jit_solution(2946073286124960940)
XLA Ops:
  0.6 90.0 %shard_map.119 = (bf16[64,3584]{1,0:T(8,128)(2,1)S(1)}, f32[64,3584]{1,0:T(8,128)S(1)}, f32[512,512]{1,0:T(8,128)S(1)}, f32[512,512]{1,0:T(8,128)S(1)}, f32[512,512]{1,0:T(8,128)S(1)}) custom-call(s32[1,56]{1,0:T(1,128)} %tgt_hbm.1, bf16[64,3584]{1,0:T(8,128)(2,1)} %grad_hbm.1, f32[64,3584]{1,0:T(8,128)} %first_hbm.1, f32[512,512]{1,0:T(8,128)} %bitcast.8, ...), custom_call_target="tpu_custom_call" | custom-call | flops 2147483648 | bytes 12582912 | tf_op jit(solution)/shard_map/pallas_call | solution.py:528
  90.7 2.2 %shard_map.120 = (bf16[64,3584]{1,0:T(8,128)(2,1)}, f32[64,3584]{1,0:T(8,128)}, f32[512,512]{1,0:T(8,128)}, f32[512,512]{1,0:T(8,128)}, f32[512,512]{1,0:T(8,128)}) custom-call(bf16[64,3584]{1,0:T(8,128)(2,1)S(1)} %get-tuple-element.15.refs_0_, f32[64,3584]{1,0:T(8,128)S(1)} %get-tuple-element.16.refs_1_, f32[512,512]{1,0:T(8,128)S(1)} %get-tuple-element.17.refs_2_, ...), custom_call_target="tpu_custom_call" | custom-call | tf_op jit(solution)/shard_map/pallas_call | solution.py:589

commit v3 on v2

v3 whole, which is shorter than its diff:
```python
import functools
import math

import jax
import jax.numpy as jnp
from jax import lax
from jax.experimental import pallas as pl
from jax.experimental.pallas import tpu as pltpu
from jax.sharding import PartitionSpec as P

CLIP_RMS = 0.5
FIRST_DECAY = 0.9
GRAM_DECAY = 0.95
GRAM_RATE = 0.05
SECOND_DECAY = 0.95
SECOND_RATE = 0.05
EPSILON = 1e-08

MESH = pl.DeviceIdType.MESH
NX, NZ, NC = 4, 8, 2
HALF = NZ // 2
COLBLK = 7
SLOTS = NX * NC
LOCAL = NX * COLBLK
ROWS = 64
BLOCK = 512
LANE = BLOCK // NX
CHUNKS = 4
FOLD = 2
DIRECT = 1
RC = ROWS // CHUNKS
Z_ORDER = (4, 5, 3, 6, 2, 7, 1)
X_ORDER = (2, 1, 3)

UNIT = RC * LANE * 2
PLAIN = [(a, r) for a in range(2) for r in range(FOLD)]
LATER = [(1, r) for r in range(FOLD, CHUNKS)] + [(2, 0), (2, 1)]
RECV = [(k,) + ar for k in "xz" for ar in PLAIN + LATER]
RECV += [("g",) + ar for ar in PLAIN + [(2, 1)]]
RECV += [("f", i) for i in range(8)] + [("n", i) for i in range(3)]

BF16, F32 = jnp.bfloat16, jnp.float32


def mm(a, b):
    return jnp.dot(a, b, preferred_element_type=F32)


def kernel(
    n_entries,
    tgt_hbm,
    grad_hbm,
    first_hbm,
    lg_hbm,
    rg_hbm,
    ql_hbm,
    qr_hbm,
    sm_hbm,
    out_v,
    f_v,
    lg_v,
    rg_v,
    sm_v,
    g_v,
    ql_v,
    qr_v,
    qlt_v,
    qrt_v,
    den_v,
    norm_s,
    norm_y,
    norm_x,
    norm_z,
    xs,
    xr,
    zs,
    zr,
    gs,
    gr,
    fx,
    fs,
    fr,
    fzs,
    fz,
    fg,
    blk,
    ms,
    mx,
    mzs,
    mz,
    uds,
    udz,
    udp,
    udx,
    fub,
    fug,
    fuz,
    fus,
    fuf,
    fsw,
    fsr,
    ub,
    ug,
    uz,
    us,
    uf,
    tgt_s,
    tgt_v,
    tbl_v,
    tbl,
    units,
    in_sem,
    send_sem,
    recv_sem,
):
    f = lax.axis_index("fsdp")
    q = lax.axis_index("mp")
    c = lax.rem(f, NC)
    z = lax.rem(f // NC, NZ)
    x = f // (NC * NZ)
    side_here = z // HALF
    n_mp = lax.axis_size("mp")

    def fid(xx, zz, cc):
        return (xx * NZ + zz) * NC + cc

    def rot(v, d, n):
        return lax.rem(v + d, n)

    near = [(dx, dc) for dx in X_ORDER + (0,) for dc in range(NC) if dx or dc]
    barrier = pltpu.get_barrier_semaphore()
    peers = [(fid(x, rot(z, d, NZ), rot(c, dc, NC)), q) for d in Z_ORDER for dc in range(NC)]
    peers += [(fid(rot(x, dx, NX), z, rot(c, dc, NC)), q) for dx, dc in near]
    peers += [(f, rot(q, d, n_mp)) for d in range(1, n_mp)]
    for peer in peers:
        pl.semaphore_signal(barrier, inc=1, device_id=peer, device_id_type=MESH)

    tgt_loads = [
        pltpu.make_async_copy(tgt_hbm, tgt_s, in_sem.at[3]),
        pltpu.make_async_copy(tgt_hbm, tgt_v, in_sem.at[4]),
    ]
    loads = [
        pltpu.make_async_copy(src, dst, in_sem.at[min(i, 2)])
        for i, (src, dst) in enumerate(
            (
                (grad_hbm, g_v),
                (first_hbm, f_v),
                (ql_hbm, ql_v),
                (qr_hbm, qr_v),
                (sm_hbm, sm_v),
                (lg_hbm, lg_v),
                (rg_hbm, rg_v),
            )
        )
    ]
    for load in loads[:1] + tgt_loads + loads[1:]:
        load.start()

    loads[0].wait()
    wide = g_v[...].astype(F32)
    cols = jnp.sum((wide * wide).reshape(ROWS // 8, 8, wide.shape[1]), axis=0)
    acc = cols[:, :128]
    for i in range(1, cols.shape[1] // 128):
        acc = acc + cols[:, i * 128 : (i + 1) * 128]
    norm_s[0] = acc
    norm_z[z] = acc

    with jax.named_scope("barrier"):
        pl.semaphore_wait(barrier, len(peers))

    sent = [0, 0, 0]
    group = [0]

    def send(src, dst, rsem, pf, pq=q, under=None):
        under = group[0] if under is None else under
        sent[under] += math.prod(src.shape) * src.dtype.itemsize // UNIT
        pltpu.make_async_remote_copy(
            src_ref=src,
            dst_ref=dst,
            send_sem=send_sem.at[under],
            recv_sem=rsem,
            device_id=(pf, pq),
            device_id_type=MESH,
        ).start()

    def recv(*key):
        return recv_sem.at[RECV.index(key)]

    def wait_units(n, sem):
        wait_bytes(units.at[pl.ds(0, n)], sem)

    def wait_bytes(ref, sem):
        pltpu.make_async_copy(ref, ref, sem).wait()

    def some(ref, n):
        return ref.at[pl.ds(0, n)]

    def all_but_one(ref):
        return some(ref, ref.shape[0] - 1)

    def p_spread(a, r, rows):
        for xx in range(NX):
            for j in range(COLBLK):
                lo = j * BLOCK + xx * LANE
                xs[a, r, xx, j] = rows[:, lo : lo + LANE]
        for d in X_ORDER:
            px = rot(x, d, NX)
            send(xs.at[a, r, px], xr[a][r].at[x], recv("x", a, r), fid(px, z, c))
        xr[a][r][x] = xs[a, r, x]

    def p_exchange(a, r):
        with jax.named_scope("p_spread_wait"):
            wait_bytes(all_but_one(xr[a][r]), recv("x", a, r))

        def slots(pz, dst):
            for s in range(SLOTS):
                l = tbl[0, fid(s // NC, pz, s % NC)]
                dst[s] = xr[a][r][l // COLBLK, lax.rem(l, COLBLK)]

        for d in Z_ORDER:
            pz = rot(z, d, NZ)
            slots(pz, zs.at[a, r, pz])
            send(zs.at[a, r, pz], zr[a][r].at[z], recv("z", a, r), fid(x, pz, c))
        slots(z, zr[a][r].at[z])

    def p_gather(a, r):
        with jax.named_scope("p_exchange_wait"):
            wait_bytes(all_but_one(zr[a][r]), recv("z", a, r))
        for s in range(SLOTS):
            h = tbl[1, fid(s // NC, z, s % NC)]
            for i in range(HALF):
                gs[a, r, s, i] = zr[a][r][h * HALF + i, s]
        for dx, dc in near:
            px, pc = rot(x, dx, NX), rot(c, dc, NC)
            send(
                gs.at[a, r, px * NC + pc],
                gr.at[a, r, x, c],
                recv("g", a, r),
                fid(px, z, pc),
            )
        gr[a, r, x, c] = gs[a, r, x * NC + c]

    def p_assemble(a, r):
        with jax.named_scope("p_gather_wait"):
            wait_bytes(all_but_one(gs.at[a, r]), recv("g", a, r))
        for xx in range(NX):
            for cc in range(NC):
                for i in range(HALF):
                    blk[a, i * NC + cc, r * RC : (r + 1) * RC, xx * LANE : (xx + 1) * LANE] = gr[
                        a, r, xx, cc, i
                    ]

    mate = fid(x, rot(z, HALF, NZ), c)

    def f_swap():
        src = g_v.at[pl.ds(pl.multiple_of((FOLD + 1 - side_here) * RC, RC), RC), :]
        send(src, fx, recv("f", 0), mate)

    def f_spread():
        with jax.named_scope("f_swap_wait"):
            wait_bytes(fx, recv("f", 0))
        mine = g_v[pl.ds(pl.multiple_of((FOLD + side_here) * RC, RC), RC), :]
        theirs = fx[...]
        for xx in range(NX):
            for j in range(COLBLK):
                lo = j * BLOCK + xx * LANE
                fs[xx, side_here, j] = mine[:, lo : lo + LANE]
                fs[xx, 1 - side_here, j] = theirs[:, lo : lo + LANE]
        for d in X_ORDER:
            px = rot(x, d, NX)
            for h in range(2):
                send(
                    fs.at[px, h],
                    fr.at[pl.ds((x * 2 + h) * COLBLK, COLBLK)],
                    recv("f", 1),
                    fid(px, z, c),
                )
        for h in range(2):
            fr[pl.ds((x * 2 + h) * COLBLK, COLBLK)] = fs[x, h]

    def f_exchange():
        with jax.named_scope("f_spread_wait"):
            wait_bytes(some(fr, 2 * COLBLK * (NX - 1)), recv("f", 1))

        def slots(pz, dst):
            for s in range(SLOTS):
                dst[s] = fr[tbl[3, fid(s // NC, pz, s % NC)]]

        for d in Z_ORDER:
            pz = rot(z, d, NZ)
            slots(pz, fzs.at[pz])
            send(fzs.at[pz], fz.at[z], recv("f", 2), fid(x, pz, c))
        slots(z, fz.at[z])

    def f_gather():
        with jax.named_scope("f_exchange_wait"):
            wait_bytes(all_but_one(fz), recv("f", 2))
        for dx, dc in near:
            px, pc = rot(x, dx, NX), rot(c, dc, NC)
            send(fz.at[:, px * NC + pc], fg.at[x, c], recv("f", 3), fid(px, z, pc))
        for i in range(NZ):
            fg[x, c, i] = fz[i, x * NC + c]

    def f_assemble():
        with jax.named_scope("f_gather_wait"):
            wait_bytes(some(fz, NZ - 1), recv("f", 3))
        for xx in range(NX):
            for cc in range(NC):
                for i in range(NZ):
                    lo = (FOLD + i // HALF) * RC
                    blk[0, i % HALF * NC + cc, lo : lo + RC, xx * LANE : (xx + 1) * LANE] = fg[
                        xx, cc, i
                    ]

    def m_spread(r):
        for d in X_ORDER:
            send(ms.at[r], mx[r].at[x], recv("x", 1, FOLD + r), fid(rot(x, d, NX), z, c))
        mx[r][x] = ms[r]

    def m_exchange(r):
        with jax.named_scope("m_spread_wait"):
            wait_bytes(all_but_one(mx[r]), recv("x", 1, FOLD + r))

        def slot(pz, pc, dst):
            l = tbl[0, fid(x, pz, pc)]
            dst[...] = mx[r][l // COLBLK, lax.rem(l, COLBLK)]

        for d in Z_ORDER + (0,):
            pz = rot(z, d, NZ)
            for dc in range(NC):
                pc = rot(c, dc, NC)
                if d or dc:
                    slot(pz, pc, mzs.at[r, pz * NC + pc])
                    send(
                        mzs.at[r, pz * NC + pc],
                        mz[r].at[z * NC + c],
                        recv("z", 1, FOLD + r),
                        fid(x, pz, pc),
                    )
        slot(z, c, mz[r].at[z * NC + c])


    def m_assemble(r):
        with jax.named_scope("m_exchange_wait"):
            wait_bytes(all_but_one(mz[r]), recv("z", 1, FOLD + r))
        h = tbl[1, f]
        for i in range(HALF):
            for cc in range(NC):
                lo = (FOLD + r) * RC
                blk[1, i * NC + cc, lo : lo + RC, :] = mz[r][(h * HALF + i) * NC + cc]

    def d_exchange(r, upd):
        for i in range(HALF):
            for cc in range(NC):
                lo = (i * NC + cc) * RC
                uds[r, i, cc] = upd[lo : lo + RC, :]
        for d in Z_ORDER + (0,):
            pz = rot(z, d, NZ)
            for dc in range(NC):
                pc = rot(c, dc, NC)
                if d or dc:
                    send(
                        uds.at[r, lax.rem(pz, HALF), pc],
                        udz[r].at[z * NC + c],
                        recv("z", 2, r),
                        fid(x, pz, pc),
                    )
        udz[r][z * NC + c] = uds[r, lax.rem(z, HALF), c]

    def d_gather(r):
        with jax.named_scope("d_exchange_wait"):
            wait_bytes(all_but_one(udz[r]), recv("z", 2, r))
        for d in X_ORDER + (0,):
            px = rot(x, d, NX)
            for j in range(COLBLK):
                t = tgt_s[0, (px * 2 + side_here) * COLBLK + j]
                part = udz[r][lax.rem(t, NZ * NC)]
                if d:
                    udp[r, px, j] = part
                else:
                    udx[r][x, j] = part
            if d:
                send(udp.at[r, px], udx[r].at[x], recv("x", 2, r), fid(px, z, c))

    def d_finish(r):
        with jax.named_scope("d_gather_wait"):
            wait_bytes(all_but_one(udx[r]), recv("x", 2, r))
        for j in range(COLBLK):
            t = tgt_s[0, (x * 2 + side_here) * COLBLK + j]
            out_v[r * RC : (r + 1) * RC, j * BLOCK : (j + 1) * BLOCK] = udx[r][t // (NZ * NC), j]

    me = x * NC + c

    def u_spread(r, upd):
        for xx in range(NX):
            for cc in range(NC):
                for i in range(HALF):
                    lo = (i * NC + cc) * RC
                    ub[r, xx, cc, i] = upd[lo : lo + RC, xx * LANE : (xx + 1) * LANE]
        for dx, dc in near:
            px, pc = rot(x, dx, NX), rot(c, dc, NC)
            send(ub.at[r, px, pc], ug.at[r, me], recv("g", 2, r), fid(px, z, pc))
        ug[r, me] = ub[r, x, c]

    def u_exchange(r):
        with jax.named_scope("u_spread_wait"):
            wait_bytes(all_but_one(ug.at[r]), recv("g", 2, r))
        for d in Z_ORDER:
            pz = rot(z, d, NZ)
            send(
                ug.at[r, :, lax.rem(pz, HALF)],
                uz[r].at[z],
                recv("z", 2, r),
                fid(x, pz, c),
            )
        for s in range(SLOTS):
            uz[r][z, s] = ug[r, s, lax.rem(z, HALF)]

    def u_gather(r):
        with jax.named_scope("u_exchange_wait"):
            wait_bytes(all_but_one(uz[r]), recv("z", 2, r))
        for d in X_ORDER + (0,):
            px = rot(x, d, NX)
            for j in range(COLBLK):
                t = tgt_s[0, (px * 2 + side_here) * COLBLK + j]
                slot = (t // (NC * NZ)) * NC + lax.rem(t, NC)
                part = uz[r][lax.rem(t // NC, NZ), slot]
                if d:
                    us[r, px, j] = part
                else:
                    uf[r, x, j] = part
            if d:
                send(us.at[r, px], uf.at[r, x], recv("x", 2, r), fid(px, z, c))

    def u_finish(r):
        with jax.named_scope("u_gather_wait"):
            wait_bytes(all_but_one(uf.at[r]), recv("x", 2, r))
        for xx in range(NX):
            for j in range(COLBLK):
                lo = j * BLOCK + xx * LANE
                out_v[r * RC : (r + 1) * RC, lo : lo + LANE] = uf[r, xx, j]

    def uf_spread(upds):
        for h in range(2):
            for xx in range(NX):
                for cc in range(NC):
                    for i in range(HALF):
                        lo = (i * NC + cc) * RC
                        fub[xx, cc, h * HALF + i] = upds[h][
                            lo : lo + RC, xx * LANE : (xx + 1) * LANE
                        ]
        for dx, dc in near:
            px, pc = rot(x, dx, NX), rot(c, dc, NC)
            send(fub.at[px, pc], fug.at[me], recv("f", 4), fid(px, z, pc))
        fug[me] = fub[x, c]

    def uf_exchange():
        with jax.named_scope("uf_spread_wait"):
            wait_bytes(all_but_one(fug), recv("f", 4))
        for d in Z_ORDER:
            pz = rot(z, d, NZ)
            send(fug.at[:, pz], fuz.at[z], recv("f", 5), fid(x, pz, c), under=2)
        for s in range(SLOTS):
            fuz[z, s] = fug[s, z]

    def uf_gather():
        with jax.named_scope("uf_exchange_wait"):
            wait_bytes(all_but_one(fuz), recv("f", 5))
        for d in X_ORDER + (0,):
            px = rot(x, d, NX)
            for h in range(2):
                for j in range(COLBLK):
                    t = tgt_s[0, (px * 2 + h) * COLBLK + j]
                    slot = (t // (NC * NZ)) * NC + lax.rem(t, NC)
                    part = fuz[lax.rem(t // NC, NZ), slot]
                    if d:
                        fus[px, h, j] = part
                    else:
                        fuf[x, h, j] = part
            if d:
                send(fus.at[px], fuf.at[x], recv("f", 6), fid(px, z, c))

    def uf_swap():
        with jax.named_scope("uf_gather_wait"):
            wait_bytes(all_but_one(fuf), recv("f", 6))
        for xx in range(NX):
            for j in range(COLBLK):
                lo = j * BLOCK + xx * LANE
                fsw[:, lo : lo + LANE] = fuf[xx, 1 - side_here, j]
        send(fsw, fsr, recv("f", 7), mate)
        rows = pl.ds(pl.multiple_of((FOLD + side_here) * RC, RC), RC)
        for xx in range(NX):
            for j in range(COLBLK):
                lo = j * BLOCK + xx * LANE
                out_v[rows, lo : lo + LANE] = fuf[xx, side_here, j]

    def uf_finish():
        with jax.named_scope("uf_swap_wait"):
            wait_bytes(fsr, recv("f", 7))
        out_v[pl.ds(pl.multiple_of((FOLD + 1 - side_here) * RC, RC), RC), :] = fsr[...]

    for d in Z_ORDER:
        send(norm_s.at[0], norm_z.at[z], recv("n", 0), fid(x, rot(z, d, NZ), c))
    p_spread(0, 0, g_v[:RC, :])
    f_swap()
    p_spread(0, 1, g_v[RC : 2 * RC, :])

    for load in tgt_loads:
        load.wait()
    n_blocks = tgt_v.shape[1]
    sub = lax.broadcasted_iota(jnp.int32, (n_blocks, 128), 0)
    lane = lax.broadcasted_iota(jnp.int32, (n_blocks, 128), 1)
    sub_sq = lax.broadcasted_iota(jnp.int32, (n_blocks, n_blocks), 0)
    lane_sq = lax.broadcasted_iota(jnp.int32, (n_blocks, n_blocks), 1)
    diag = jnp.where(sub_sq == lane_sq, jnp.broadcast_to(tgt_v[...], sub_sq.shape), 0)
    named = jnp.sum(diag, axis=1, keepdims=True) == lane
    band = sub // COLBLK
    side = lax.rem(band, 2)
    local = jnp.where(side == side_here, sub - (band - band // 2) * COLBLK, 0)
    for i, code in enumerate((local, side, jnp.ones_like(sub), sub)):
        tbl_v[i : i + 1, :] = jnp.max(jnp.where(named, code, 0), axis=0, keepdims=True)
    tbl_copy = pltpu.make_async_copy(tbl_v, tbl, in_sem.at[5])
    tbl_copy.start()

    with jax.named_scope("norm_z_wait"):
        wait_bytes(all_but_one(norm_z), recv("n", 0))
    acc = jnp.sum(norm_z[...], axis=0)
    norm_s[1] = acc
    norm_y[q] = acc
    for d in range(1, n_mp):
        send(norm_s.at[1], norm_y.at[q], recv("n", 1), f, rot(q, d, n_mp))
    tbl_copy.wait()
    p_exchange(0, 0)
    with jax.named_scope("norm_y_wait"):
        wait_bytes(all_but_one(norm_y), recv("n", 1))
    acc = jnp.sum(norm_y[...], axis=0)
    norm_s[2] = acc
    norm_x[me] = acc
    for dx, dc in near:
        send(
            norm_s.at[2],
            norm_x.at[me],
            recv("n", 2),
            fid(rot(x, dx, NX), z, rot(c, dc, NC)),
        )
    p_exchange(0, 1)
    f_spread()
    with jax.named_scope("norm_x_wait"):
        wait_bytes(all_but_one(norm_x), recv("n", 2))
    acc = jnp.sum(norm_x[...], axis=0)
    norm_sum = jnp.sum(jnp.sum(acc, axis=0, keepdims=True), axis=1, keepdims=True)
    clip = jnp.minimum(1.0, CLIP_RMS * (float(n_entries) ** 0.5) / jnp.sqrt(norm_sum))

    loads[1].wait()
    for r in range(CHUNKS):
        rows = slice(r * RC, (r + 1) * RC)
        nxt = FIRST_DECAY * f_v[rows, :] + ((1.0 - FIRST_DECAY) * clip) * g_v[rows, :].astype(F32)
        f_v[rows, :] = nxt
        low = nxt.astype(BF16)
        if r < FOLD:
            p_spread(1, r, low)
        else:
            for j in range(COLBLK):
                ms[r - FOLD, j] = low[:, j * BLOCK : (j + 1) * BLOCK]
            m_spread(r - FOLD)
    wait_units(1024, in_sem.at[2])
    qlt_v[...] = ql_v[...].reshape(BLOCK, BLOCK).T
    qrt_v[...] = qr_v[...].T
    f_exchange()
    p_exchange(1, 0)
    p_exchange(1, 1)
    p_gather(0, 0)
    m_exchange(0)
    p_gather(0, 1)
    f_gather()
    m_exchange(1)

    for r in range(FOLD):
        p_assemble(0, r)
    f_assemble()
    with jax.named_scope("owner_gradient"):
        live = tbl[2, f] > 0
        block = blk[0].reshape(BLOCK, BLOCK)
        half = mm(qlt_v[...], block).astype(BF16)
        rotated = clip * mm(half, qr_v[...])
        second = SECOND_DECAY * sm_v[...] + SECOND_RATE * rotated * rotated
        den_v[...] = jnp.sqrt(second) + EPSILON
        sm_v[...] = jnp.where(live, second, sm_v[...])
        scale = GRAM_RATE * clip * clip / BLOCK
        block_t = block.T
        lg_v[...] = jnp.where(live, GRAM_DECAY * lg_v[...] + scale * mm(block, block_t), lg_v[...])
        rg_v[...] = jnp.where(live, GRAM_DECAY * rg_v[...] + scale * mm(block_t, block), rg_v[...])

    for r in range(FOLD):
        p_gather(1, r)
    for r in range(FOLD):
        p_assemble(1, r)
    for r in range(CHUNKS - FOLD):
        m_assemble(r)
    with jax.named_scope("owner_moment"):
        mhalf = mm(qlt_v[...], blk[1].reshape(BLOCK, BLOCK)).astype(BF16)
        normed = (mm(mhalf, qr_v[...]) / den_v[...]).astype(BF16)

    def update(r):
        rows = ql_v[:, r * RC : (r + 1) * RC, :].reshape(HALF * NC * RC, BLOCK)
        return mm(mm(rows, normed).astype(BF16), qrt_v[...]).astype(BF16)

    group[0] = 1
    d_exchange(0, update(0))
    uf_spread([update(FOLD), update(FOLD + 1)])
    upd = update(1)

    wait_units(sent[0], send_sem.at[0])

    uf_exchange()
    u_spread(1, upd)
    d_gather(0)
    with jax.named_scope("uf_sent_wait"):
        wait_units(sent[2], send_sem.at[2])
    u_exchange(1)
    uf_gather()
    uf_swap()
    u_gather(1)
    d_finish(0)
    u_finish(1)
    uf_finish()
    wait_units(sent[1], send_sem.at[1])


def write_out(*refs):
    n = (len(refs) - 1) // 2
    copies = [
        pltpu.make_async_copy(refs[i], refs[n + i], refs[-1].at[i]) for i in range(n)
    ]
    for copy in copies:
        copy.start()
    for copy in copies:
        copy.wait()


def shards(
    gradient,
    first_moment,
    left_gram,
    right_gram,
    left_basis,
    right_basis,
    second_moment,
    block_target,
):
    rows, cols = gradient.shape
    n_fsdp = lax.axis_size("fsdp")
    n_mp = lax.axis_size("mp")
    n_blocks = block_target.shape[1]
    any_spec = pl.BlockSpec(memory_space=pl.ANY)
    vmem_spec = pl.BlockSpec(memory_space=pltpu.VMEM)
    vm = pltpu.VMEM
    dma = pltpu.SemaphoreType.DMA
    mat = (BLOCK, BLOCK)
    piece = (RC, LANE)
    strip = (RC, BLOCK)

    def per_chunk(n, *shape):
        return [vm(shape, BF16) for _ in range(n)]

    shapes = [((rows, cols), BF16), ((rows, cols), F32)] + [(mat, F32)] * 3
    held = pl.pallas_call(
        functools.partial(kernel, rows * cols * n_fsdp * n_mp),
        out_shape=tuple(vm(s, d) for s, d in shapes),
        in_specs=[any_spec] * 8,
        out_specs=(vmem_spec,) * 5,
        scratch_shapes=[
            vm((rows, cols), BF16),
            vm((HALF * NC, ROWS, BLOCK), BF16),
            vm(mat, BF16),
            vm(mat, BF16),
            vm(mat, BF16),
            vm(mat, F32),
            vm((3, 8, 128), F32),
            vm((n_mp, 8, 128), F32),
            vm((SLOTS, 8, 128), F32),
            vm((NZ, 8, 128), F32),
            vm((2, FOLD, NX, COLBLK) + piece, BF16),
            [per_chunk(FOLD, NX, COLBLK, *piece) for _ in range(2)],
            vm((2, FOLD, NZ, SLOTS) + piece, BF16),
            [per_chunk(FOLD, NZ, SLOTS, *piece) for _ in range(2)],
            vm((2, FOLD, SLOTS, HALF) + piece, BF16),
            vm((2, FOLD, NX, NC, HALF) + piece, BF16),
            vm((RC, cols), BF16),
            vm((NX, 2, COLBLK) + piece, BF16),
            vm((2 * LOCAL,) + piece, BF16),
            vm((NZ, SLOTS) + piece, BF16),
            vm((NZ, SLOTS) + piece, BF16),
            vm((NX, NC, NZ) + piece, BF16),
            vm((2, HALF * NC, ROWS, BLOCK), BF16),
            vm((CHUNKS - FOLD, COLBLK) + strip, BF16),
            per_chunk(CHUNKS - FOLD, NX, COLBLK, *strip),
            vm((CHUNKS - FOLD, NZ * NC) + strip, BF16),
            per_chunk(CHUNKS - FOLD, NZ * NC, *strip),
            vm((DIRECT, HALF, NC) + strip, BF16),
            per_chunk(DIRECT, NZ * NC, *strip),
            vm((DIRECT, NX, COLBLK) + strip, BF16),
            per_chunk(DIRECT, NX, COLBLK, *strip),
            vm((NX, NC, NZ) + piece, BF16),
            vm((SLOTS, NZ) + piece, BF16),
            vm((NZ, SLOTS) + piece, BF16),
            vm((NX, 2, COLBLK) + piece, BF16),
            vm((NX, 2, COLBLK) + piece, BF16),
            vm((RC, cols), BF16),
            vm((RC, cols), BF16),
            vm((CHUNKS, NX, NC, HALF) + piece, BF16),
            vm((CHUNKS, SLOTS, HALF) + piece, BF16),
            per_chunk(CHUNKS, NZ, SLOTS, *piece),
            vm((CHUNKS, NX, COLBLK) + piece, BF16),
            vm((CHUNKS, NX, COLBLK) + piece, BF16),
            pltpu.SMEM((1, n_blocks), jnp.int32),
            vm((1, n_blocks), jnp.int32),
            vm((8, 128), jnp.int32),
            pltpu.SMEM((8, 128), jnp.int32),
            vm((1024, RC, LANE), BF16),
            dma((6,)),
            dma((3,)),
            dma((len(RECV),)),
        ],
        compiler_params=pltpu.CompilerParams(
            collective_id=0, has_side_effects=True, vmem_limit_bytes=59 * 2**20
        ),
        cost_estimate=pl.CostEstimate(
            flops=16 * BLOCK**3, bytes_accessed=12 * 2**20, transcendentals=BLOCK**2
        ),
    )(
        block_target,
        gradient,
        first_moment,
        left_gram[0, 0],
        right_gram[0, 0],
        left_basis[0, 0].reshape(HALF * NC, ROWS, BLOCK),
        right_basis[0, 0],
        second_moment[0, 0],
    )
    out = pl.pallas_call(
        write_out,
        out_shape=tuple(jax.ShapeDtypeStruct(s, d) for s, d in shapes),
        in_specs=[vmem_spec] * 5,
        out_specs=(any_spec,) * 5,
        scratch_shapes=[dma((5,))],
        compiler_params=pltpu.CompilerParams(vmem_limit_bytes=2**20),
    )(*held)
    return (out[0], out[1]) + tuple(o[None, None] for o in out[2:])


def solution(mesh):
    return jax.shard_map(
        shards,
        mesh=mesh,
        in_specs=(
            P("fsdp", "mp"),
            P("fsdp", "mp"),
            P("fsdp", "mp", None, None),
            P("fsdp", "mp", None, None),
            P("fsdp", "mp", None, None),
            P("fsdp", "mp", None, None),
            P("fsdp", "mp", None, None),
            P("mp", None),
        ),
        out_specs=(
            P("fsdp", "mp"),
            P("fsdp", "mp"),
            P("fsdp", "mp", None, None),
            P("fsdp", "mp", None, None),
            P("fsdp", "mp", None, None),
        ),
        check_vma=False,
    )
```

time: 93.2 us -> 89 us (0.955)
  Pallas kernels: 92.2 us -> 88.3 us
    pallas_call x1, Pallas kernels: 90 us -> 86.1 us  [shards(): pl.pallas_call(functools.partial(kernel, rows * cols * n_fsdp * n_mp), ou...]
where the time goes in v3:
time: 89 us; the launch traced here: 88.9 us
  Pallas kernels  88.3 us (99%)
    pallas_call x1, Pallas kernels, shards(): pl.pallas_call(functools.partial(kernel, rows * cols * n_fsdp * n_mp), ou...  86.1 us
    pallas_call x1, Pallas kernels, shards(): pl.pallas_call(write_out, out_shape=tuple((jax.ShapeDtypeStruct(s, d) for...  2.16 us

profile of v3, /device:TPU:1, one launch (start us, length us, event | category | flops | bytes accessed | tf_op | source)
XLA Modules:
  0.0 88.9 jit_solution(10752658661106363905)
XLA Ops:
  0.6 86.1 %shard_map.119 = (bf16[64,3584]{1,0:T(8,128)(2,1)S(1)}, f32[64,3584]{1,0:T(8,128)S(1)}, f32[512,512]{1,0:T(8,128)S(1)}, f32[512,512]{1,0:T(8,128)S(1)}, f32[512,512]{1,0:T(8,128)S(1)}) custom-call(s32[1,56]{1,0:T(1,128)} %tgt_hbm.1, bf16[64,3584]{1,0:T(8,128)(2,1)} %grad_hbm.1, f32[64,3584]{1,0:T(8,128)} %first_hbm.1, f32[512,512]{1,0:T(8,128)} %bitcast.8, ...), custom_call_target="tpu_custom_call" | custom-call | flops 2147483648 | bytes 12582912 | tf_op jit(solution)/shard_map/pallas_call | solution.py:667
  86.8 2.2 %shard_map.120 = (bf16[64,3584]{1,0:T(8,128)(2,1)}, f32[64,3584]{1,0:T(8,128)}, f32[512,512]{1,0:T(8,128)}, f32[512,512]{1,0:T(8,128)}, f32[512,512]{1,0:T(8,128)}) custom-call(bf16[64,3584]{1,0:T(8,128)(2,1)S(1)} %get-tuple-element.15.refs_0_, f32[64,3584]{1,0:T(8,128)S(1)} %get-tuple-element.16.refs_1_, f32[512,512]{1,0:T(8,128)S(1)} %get-tuple-element.17.refs_2_, ...), custom_call_target="tpu_custom_call" | custom-call | tf_op jit(solution)/shard_map/pallas_call | solution.py:741

commit v4 on v3

--- a/solution.py
+++ b/solution.py
@@ -37,7 +37,7 @@
 LATER = [(1, r) for r in range(FOLD, CHUNKS)] + [(2, 0), (2, 1)]
 RECV = [(k,) + ar for k in "xz" for ar in PLAIN + LATER]
 RECV += [("g",) + ar for ar in PLAIN + [(2, 1)]]
-RECV += [("f", i) for i in range(8)] + [("n", i) for i in range(3)]
+RECV += [("f", i) for i in range(9) if i != 6] + [("s", d) for d in X_ORDER] + [("n", i) for i in range(3)]
 
 BF16, F32 = jnp.bfloat16, jnp.float32
 
@@ -97,7 +97,6 @@
     fuz,
     fus,
     fuf,
-    fsw,
     fsr,
     ub,
     ug,
@@ -466,38 +465,50 @@
     def uf_gather():
         with jax.named_scope("uf_exchange_wait"):
             wait_bytes(all_but_one(fuz), recv("f", 5))
-        for d in X_ORDER + (0,):
-            px = rot(x, d, NX)
-            for h in range(2):
+        for i, h in enumerate((1 - side_here, side_here)):
+            for d in X_ORDER + (0,):
+                px = rot(x, d, NX)
                 for j in range(COLBLK):
                     t = tgt_s[0, (px * 2 + h) * COLBLK + j]
                     slot = (t // (NC * NZ)) * NC + lax.rem(t, NC)
                     part = fuz[lax.rem(t // NC, NZ), slot]
                     if d:
-                        fus[px, h, j] = part
+                        fus[h, px, j] = part
                     else:
-                        fuf[x, h, j] = part
+                        fuf[h, x, j] = part
+                if d:
+                    send(
+                        fus.at[h, px],
+                        fuf.at[h, x],
+                        recv("s", d) if i == 0 else recv("f", 8),
+                        fid(px, z, c),
+                    )
+
+    def uf_swap():
+        for d in (0,) + X_ORDER[1:] + X_ORDER[:1]:
+            xx = rot(x, NX - d, NX)
+            piece = fuf.at[1 - side_here, xx]
             if d:
-                send(fus.at[px], fuf.at[x], recv("f", 6), fid(px, z, c))
-
-    def uf_swap():
-        with jax.named_scope("uf_gather_wait"):
-            wait_bytes(all_but_one(fuf), recv("f", 6))
-        for xx in range(NX):
-            for j in range(COLBLK):
-                lo = j * BLOCK + xx * LANE
-                fsw[:, lo : lo + LANE] = fuf[xx, 1 - side_here, j]
-        send(fsw, fsr, recv("f", 7), mate)
+                with jax.named_scope("uf_gather_wait"):
+                    wait_bytes(piece, recv("s", d))
+            send(piece, fsr.at[xx], recv("f", 7), mate)
+
+    def uf_keep():
+        wait_bytes(some(fuf.at[0], NX - 1), recv("f", 8))
         rows = pl.ds(pl.multiple_of((FOLD + side_here) * RC, RC), RC)
         for xx in range(NX):
             for j in range(COLBLK):
                 lo = j * BLOCK + xx * LANE
-                out_v[rows, lo : lo + LANE] = fuf[xx, side_here, j]
+                out_v[rows, lo : lo + LANE] = fuf[side_here, xx, j]
 
     def uf_finish():
         with jax.named_scope("uf_swap_wait"):
             wait_bytes(fsr, recv("f", 7))
-        out_v[pl.ds(pl.multiple_of((FOLD + 1 - side_here) * RC, RC), RC), :] = fsr[...]
+        rows = pl.ds(pl.multiple_of((FOLD + 1 - side_here) * RC, RC), RC)
+        for xx in range(NX):
+            for j in range(COLBLK):
+                lo = j * BLOCK + xx * LANE
+                out_v[rows, lo : lo + LANE] = fsr[xx, j]
 
     for d in Z_ORDER:
         send(norm_s.at[0], norm_z.at[z], recv("n", 0), fid(x, rot(z, d, NZ), c))
@@ -621,6 +632,7 @@
     uf_gather()
     uf_swap()
     u_gather(1)
+    uf_keep()
     d_finish(0)
     u_finish(1)
     uf_finish()
@@ -704,10 +716,9 @@
             vm((NX, NC, NZ) + piece, BF16),
             vm((SLOTS, NZ) + piece, BF16),
             vm((NZ, SLOTS) + piece, BF16),
-            vm((NX, 2, COLBLK) + piece, BF16),
-            vm((NX, 2, COLBLK) + piece, BF16),
-            vm((RC, cols), BF16),
-            vm((RC, cols), BF16),
+            vm((2, NX, COLBLK) + piece, BF16),
+            vm((2, NX, COLBLK) + piece, BF16),
+            vm((NX, COLBLK) + piece, BF16),
             vm((CHUNKS, NX, NC, HALF) + piece, BF16),
             vm((CHUNKS, SLOTS, HALF) + piece, BF16),
             per_chunk(CHUNKS, NZ, SLOTS, *piece),

time: 89 us -> 86.1 us (0.967)
  Pallas kernels: 88.3 us -> 84.6 us
    pallas_call x1, Pallas kernels: 86.1 us -> 82.5 us  [shards(): pl.pallas_call(functools.partial(kernel, rows * cols * n_fsdp * n_mp), ou...]
where the time goes in v4:
time: 86.1 us; the launch traced here: 85.3 us
  Pallas kernels  84.6 us (98%)
    pallas_call x1, Pallas kernels, shards(): pl.pallas_call(functools.partial(kernel, rows * cols * n_fsdp * n_mp), ou...  82.5 us
    pallas_call x1, Pallas kernels, shards(): pl.pallas_call(write_out, out_shape=tuple((jax.ShapeDtypeStruct(s, d) for...  2.16 us

profile of v4, /device:TPU:1, one launch (start us, length us, event | category | flops | bytes accessed | tf_op | source)
XLA Modules:
  0.0 85.3 jit_solution(9258849041579303687)
XLA Ops:
  0.6 82.5 %shard_map.119 = (bf16[64,3584]{1,0:T(8,128)(2,1)S(1)}, f32[64,3584]{1,0:T(8,128)S(1)}, f32[512,512]{1,0:T(8,128)S(1)}, f32[512,512]{1,0:T(8,128)S(1)}, f32[512,512]{1,0:T(8,128)S(1)}) custom-call(s32[1,56]{1,0:T(1,128)} %tgt_hbm.1, bf16[64,3584]{1,0:T(8,128)(2,1)} %grad_hbm.1, f32[64,3584]{1,0:T(8,128)} %first_hbm.1, f32[512,512]{1,0:T(8,128)} %bitcast.8, ...), custom_call_target="tpu_custom_call" | custom-call | flops 2147483648 | bytes 12582912 | tf_op jit(solution)/shard_map/pallas_call | solution.py:679
  83.1 2.2 %shard_map.120 = (bf16[64,3584]{1,0:T(8,128)(2,1)}, f32[64,3584]{1,0:T(8,128)}, f32[512,512]{1,0:T(8,128)}, f32[512,512]{1,0:T(8,128)}, f32[512,512]{1,0:T(8,128)}) custom-call(bf16[64,3584]{1,0:T(8,128)(2,1)S(1)} %get-tuple-element.15.refs_0_, f32[64,3584]{1,0:T(8,128)S(1)} %get-tuple-element.16.refs_1_, f32[512,512]{1,0:T(8,128)S(1)} %get-tuple-element.17.refs_2_, ...), custom_call_target="tpu_custom_call" | custom-call | tf_op jit(solution)/shard_map/pallas_call | solution.py:752

commit v5 on v4

--- a/solution.py
+++ b/solution.py
@@ -33,11 +33,11 @@
 X_ORDER = (2, 1, 3)
 
 UNIT = RC * LANE * 2
-PLAIN = [(a, r) for a in range(2) for r in range(FOLD)]
+PLAIN = [(0, r) for r in range(FOLD)]
 LATER = [(1, r) for r in range(FOLD, CHUNKS)] + [(2, 0), (2, 1)]
 RECV = [(k,) + ar for k in "xz" for ar in PLAIN + LATER]
 RECV += [("g",) + ar for ar in PLAIN + [(2, 1)]]
-RECV += [("f", i) for i in range(9) if i != 6] + [("s", d) for d in X_ORDER] + [("n", i) for i in range(3)]
+RECV += [("f", a, i) for a in range(2) for i in range(4)] + [("f", i) for i in (4, 5, 7, 8)] + [("s", d) for d in X_ORDER] + [("n", i) for i in range(3)]
 
 BF16, F32 = jnp.bfloat16, jnp.float32
 
@@ -77,6 +77,7 @@
     zr,
     gs,
     gr,
+    mf,
     fx,
     fs,
     fr,
@@ -167,7 +168,7 @@
     with jax.named_scope("barrier"):
         pl.semaphore_wait(barrier, len(peers))
 
-    sent = [0, 0, 0]
+    sent = [0, 0, 0, 0]
     group = [0]
 
     def send(src, dst, rsem, pf, pq=q, under=None):
@@ -197,118 +198,122 @@
     def all_but_one(ref):
         return some(ref, ref.shape[0] - 1)
 
-    def p_spread(a, r, rows):
+    def p_spread(r, rows):
         for xx in range(NX):
             for j in range(COLBLK):
                 lo = j * BLOCK + xx * LANE
-                xs[a, r, xx, j] = rows[:, lo : lo + LANE]
+                xs[r, xx, j] = rows[:, lo : lo + LANE]
         for d in X_ORDER:
             px = rot(x, d, NX)
-            send(xs.at[a, r, px], xr[a][r].at[x], recv("x", a, r), fid(px, z, c))
-        xr[a][r][x] = xs[a, r, x]
-
-    def p_exchange(a, r):
+            send(xs.at[r, px], xr[r].at[x], recv("x", 0, r), fid(px, z, c))
+        xr[r][x] = xs[r, x]
+
+    def p_exchange(r):
         with jax.named_scope("p_spread_wait"):
-            wait_bytes(all_but_one(xr[a][r]), recv("x", a, r))
+            wait_bytes(all_but_one(xr[r]), recv("x", 0, r))
 
         def slots(pz, dst):
             for s in range(SLOTS):
                 l = tbl[0, fid(s // NC, pz, s % NC)]
-                dst[s] = xr[a][r][l // COLBLK, lax.rem(l, COLBLK)]
+                dst[s] = xr[r][l // COLBLK, lax.rem(l, COLBLK)]
 
         for d in Z_ORDER:
             pz = rot(z, d, NZ)
-            slots(pz, zs.at[a, r, pz])
-            send(zs.at[a, r, pz], zr[a][r].at[z], recv("z", a, r), fid(x, pz, c))
-        slots(z, zr[a][r].at[z])
-
-    def p_gather(a, r):
+            slots(pz, zs.at[r, pz])
+            send(zs.at[r, pz], zr[r].at[z], recv("z", 0, r), fid(x, pz, c))
+        slots(z, zr[r].at[z])
+
+    def p_gather(r):
         with jax.named_scope("p_exchange_wait"):
-            wait_bytes(all_but_one(zr[a][r]), recv("z", a, r))
+            wait_bytes(all_but_one(zr[r]), recv("z", 0, r))
         for s in range(SLOTS):
             h = tbl[1, fid(s // NC, z, s % NC)]
             for i in range(HALF):
-                gs[a, r, s, i] = zr[a][r][h * HALF + i, s]
+                gs[r, s, i] = zr[r][h * HALF + i, s]
         for dx, dc in near:
             px, pc = rot(x, dx, NX), rot(c, dc, NC)
             send(
-                gs.at[a, r, px * NC + pc],
-                gr.at[a, r, x, c],
-                recv("g", a, r),
+                gs.at[r, px * NC + pc],
+                gr.at[r, x, c],
+                recv("g", 0, r),
                 fid(px, z, pc),
             )
-        gr[a, r, x, c] = gs[a, r, x * NC + c]
-
-    def p_assemble(a, r):
+        gr[r, x, c] = gs[r, x * NC + c]
+
+    def p_assemble(r):
         with jax.named_scope("p_gather_wait"):
-            wait_bytes(all_but_one(gs.at[a, r]), recv("g", a, r))
+            wait_bytes(all_but_one(gs.at[r]), recv("g", 0, r))
         for xx in range(NX):
             for cc in range(NC):
                 for i in range(HALF):
-                    blk[a, i * NC + cc, r * RC : (r + 1) * RC, xx * LANE : (xx + 1) * LANE] = gr[
-                        a, r, xx, cc, i
+                    blk[0, i * NC + cc, r * RC : (r + 1) * RC, xx * LANE : (xx + 1) * LANE] = gr[
+                        r, xx, cc, i
                     ]
 
     mate = fid(x, rot(z, HALF, NZ), c)
 
-    def f_swap():
-        src = g_v.at[pl.ds(pl.multiple_of((FOLD + 1 - side_here) * RC, RC), RC), :]
-        send(src, fx, recv("f", 0), mate)
-
-    def f_spread():
+    def f_swap(a, src):
+        send(src, fx.at[a], recv("f", a, 0), mate)
+
+    def f_spread(a, mine):
         with jax.named_scope("f_swap_wait"):
-            wait_bytes(fx, recv("f", 0))
-        mine = g_v[pl.ds(pl.multiple_of((FOLD + side_here) * RC, RC), RC), :]
-        theirs = fx[...]
+            wait_bytes(fx.at[a], recv("f", a, 0))
+        theirs = fx[a]
         for xx in range(NX):
             for j in range(COLBLK):
                 lo = j * BLOCK + xx * LANE
-                fs[xx, side_here, j] = mine[:, lo : lo + LANE]
-                fs[xx, 1 - side_here, j] = theirs[:, lo : lo + LANE]
+                fs[a, xx, side_here, j] = mine[:, lo : lo + LANE]
+                fs[a, xx, 1 - side_here, j] = theirs[:, lo : lo + LANE]
         for d in X_ORDER:
             px = rot(x, d, NX)
             for h in range(2):
                 send(
-                    fs.at[px, h],
-                    fr.at[pl.ds((x * 2 + h) * COLBLK, COLBLK)],
-                    recv("f", 1),
+                    fs.at[a, px, h],
+                    fr[a].at[pl.ds((x * 2 + h) * COLBLK, COLBLK)],
+                    recv("f", a, 1),
                     fid(px, z, c),
                 )
         for h in range(2):
-            fr[pl.ds((x * 2 + h) * COLBLK, COLBLK)] = fs[x, h]
-
-    def f_exchange():
+            fr[a][pl.ds((x * 2 + h) * COLBLK, COLBLK)] = fs[a, x, h]
+
+    def f_exchange(a):
         with jax.named_scope("f_spread_wait"):
-            wait_bytes(some(fr, 2 * COLBLK * (NX - 1)), recv("f", 1))
+            wait_bytes(some(fr[a], 2 * COLBLK * (NX - 1)), recv("f", a, 1))
 
         def slots(pz, dst):
             for s in range(SLOTS):
-                dst[s] = fr[tbl[3, fid(s // NC, pz, s % NC)]]
+                dst[s] = fr[a][tbl[3, fid(s // NC, pz, s % NC)]]
 
         for d in Z_ORDER:
             pz = rot(z, d, NZ)
-            slots(pz, fzs.at[pz])
-            send(fzs.at[pz], fz.at[z], recv("f", 2), fid(x, pz, c))
-        slots(z, fz.at[z])
-
-    def f_gather():
+            slots(pz, fzs.at[a, pz])
+            send(
+                fzs.at[a, pz],
+                fz.at[a, z],
+                recv("f", a, 2),
+                fid(x, pz, c),
+                under=3 if a else 0,
+            )
+        slots(z, fz.at[a, z])
+
+    def f_gather(a):
         with jax.named_scope("f_exchange_wait"):
-            wait_bytes(all_but_one(fz), recv("f", 2))
+            wait_bytes(all_but_one(fz.at[a]), recv("f", a, 2))
         for dx, dc in near:
             px, pc = rot(x, dx, NX), rot(c, dc, NC)
-            send(fz.at[:, px * NC + pc], fg.at[x, c], recv("f", 3), fid(px, z, pc))
+            send(fz.at[a, :, px * NC + pc], fg.at[a, x, c], recv("f", a, 3), fid(px, z, pc))
         for i in range(NZ):
-            fg[x, c, i] = fz[i, x * NC + c]
-
-    def f_assemble():
+            fg[a, x, c, i] = fz[a, i, x * NC + c]
+
+    def f_assemble(a, first):
         with jax.named_scope("f_gather_wait"):
-            wait_bytes(some(fz, NZ - 1), recv("f", 3))
+            wait_bytes(some(fz.at[a], NZ - 1), recv("f", a, 3))
         for xx in range(NX):
             for cc in range(NC):
                 for i in range(NZ):
-                    lo = (FOLD + i // HALF) * RC
-                    blk[0, i % HALF * NC + cc, lo : lo + RC, xx * LANE : (xx + 1) * LANE] = fg[
-                        xx, cc, i
+                    lo = (first + i // HALF) * RC
+                    blk[a, i % HALF * NC + cc, lo : lo + RC, xx * LANE : (xx + 1) * LANE] = fg[
+                        a, xx, cc, i
                     ]
 
     def m_spread(r):
@@ -512,9 +517,9 @@
 
     for d in Z_ORDER:
         send(norm_s.at[0], norm_z.at[z], recv("n", 0), fid(x, rot(z, d, NZ), c))
-    p_spread(0, 0, g_v[:RC, :])
-    f_swap()
-    p_spread(0, 1, g_v[RC : 2 * RC, :])
+    p_spread(0, g_v[:RC, :])
+    f_swap(0, g_v.at[pl.ds(pl.multiple_of((FOLD + 1 - side_here) * RC, RC), RC), :])
+    p_spread(1, g_v[RC : 2 * RC, :])
 
     for load in tgt_loads:
         load.wait()
@@ -541,7 +546,7 @@
     for d in range(1, n_mp):
         send(norm_s.at[1], norm_y.at[q], recv("n", 1), f, rot(q, d, n_mp))
     tbl_copy.wait()
-    p_exchange(0, 0)
+    p_exchange(0)
     with jax.named_scope("norm_y_wait"):
         wait_bytes(all_but_one(norm_y), recv("n", 1))
     acc = jnp.sum(norm_y[...], axis=0)
@@ -554,8 +559,8 @@
             recv("n", 2),
             fid(rot(x, dx, NX), z, rot(c, dc, NC)),
         )
-    p_exchange(0, 1)
-    f_spread()
+    p_exchange(1)
+    f_spread(0, g_v[pl.ds(pl.multiple_of((FOLD + side_here) * RC, RC), RC), :])
     with jax.named_scope("norm_x_wait"):
         wait_bytes(all_but_one(norm_x), recv("n", 2))
     acc = jnp.sum(norm_x[...], axis=0)
@@ -569,7 +574,9 @@
         f_v[rows, :] = nxt
         low = nxt.astype(BF16)
         if r < FOLD:
-            p_spread(1, r, low)
+            mf[r] = low
+            if r == FOLD - 1:
+                f_swap(1, mf.at[1 - side_here])
         else:
             for j in range(COLBLK):
                 ms[r - FOLD, j] = low[:, j * BLOCK : (j + 1) * BLOCK]
@@ -577,18 +584,17 @@
     wait_units(1024, in_sem.at[2])
     qlt_v[...] = ql_v[...].reshape(BLOCK, BLOCK).T
     qrt_v[...] = qr_v[...].T
-    f_exchange()
-    p_exchange(1, 0)
-    p_exchange(1, 1)
-    p_gather(0, 0)
+    f_exchange(0)
+    p_gather(0)
     m_exchange(0)
-    p_gather(0, 1)
-    f_gather()
-    m_exchange(1)
+    f_spread(1, mf[side_here])
+    p_gather(1)
+    f_exchange(1)
+    f_gather(0)
 
     for r in range(FOLD):
-        p_assemble(0, r)
-    f_assemble()
+        p_assemble(r)
+    f_assemble(0, FOLD)
     with jax.named_scope("owner_gradient"):
         live = tbl[2, f] > 0
         block = blk[0].reshape(BLOCK, BLOCK)
@@ -602,10 +608,11 @@
         lg_v[...] = jnp.where(live, GRAM_DECAY * lg_v[...] + scale * mm(block, block_t), lg_v[...])
         rg_v[...] = jnp.where(live, GRAM_DECAY * rg_v[...] + scale * mm(block_t, block), rg_v[...])
 
-    for r in range(FOLD):
-        p_gather(1, r)
-    for r in range(FOLD):
-        p_assemble(1, r)
+    wait_units(sent[3], send_sem.at[3])
+    m_exchange(1)
+
+    f_gather(1)
+    f_assemble(1, 0)
     for r in range(CHUNKS - FOLD):
         m_assemble(r)
     with jax.named_scope("owner_moment"):
@@ -692,18 +699,19 @@
             vm((n_mp, 8, 128), F32),
             vm((SLOTS, 8, 128), F32),
             vm((NZ, 8, 128), F32),
-            vm((2, FOLD, NX, COLBLK) + piece, BF16),
-            [per_chunk(FOLD, NX, COLBLK, *piece) for _ in range(2)],
-            vm((2, FOLD, NZ, SLOTS) + piece, BF16),
-            [per_chunk(FOLD, NZ, SLOTS, *piece) for _ in range(2)],
-            vm((2, FOLD, SLOTS, HALF) + piece, BF16),
-            vm((2, FOLD, NX, NC, HALF) + piece, BF16),
-            vm((RC, cols), BF16),
-            vm((NX, 2, COLBLK) + piece, BF16),
-            vm((2 * LOCAL,) + piece, BF16),
-            vm((NZ, SLOTS) + piece, BF16),
-            vm((NZ, SLOTS) + piece, BF16),
-            vm((NX, NC, NZ) + piece, BF16),
+            vm((FOLD, NX, COLBLK) + piece, BF16),
+            per_chunk(FOLD, NX, COLBLK, *piece),
+            vm((FOLD, NZ, SLOTS) + piece, BF16),
+            per_chunk(FOLD, NZ, SLOTS, *piece),
+            vm((FOLD, SLOTS, HALF) + piece, BF16),
+            vm((FOLD, NX, NC, HALF) + piece, BF16),
+            vm((2, RC, cols), BF16),
+            vm((2, RC, cols), BF16),
+            vm((2, NX, 2, COLBLK) + piece, BF16),
+            per_chunk(2, 2 * LOCAL, *piece),
+            vm((2, NZ, SLOTS) + piece, BF16),
+            vm((2, NZ, SLOTS) + piece, BF16),
+            vm((2, NX, NC, NZ) + piece, BF16),
             vm((2, HALF * NC, ROWS, BLOCK), BF16),
             vm((CHUNKS - FOLD, COLBLK) + strip, BF16),
             per_chunk(CHUNKS - FOLD, NX, COLBLK, *strip),
@@ -730,7 +738,7 @@
             pltpu.SMEM((8, 128), jnp.int32),
             vm((1024, RC, LANE), BF16),
             dma((6,)),
-            dma((3,)),
+            dma((4,)),
             dma((len(RECV),)),
         ],
         compiler_params=pltpu.CompilerParams(

time: 86.1 us -> 85.5 us (level)
  no operation moved by 1% of the time
where the time goes in v5:
time: 85.5 us; the launch traced here: 85.4 us
  Pallas kernels  84.7 us (99%)
    pallas_call x1, Pallas kernels, shards(): pl.pallas_call(functools.partial(kernel, rows * cols * n_fsdp * n_mp), ou...  82.6 us
    pallas_call x1, Pallas kernels, shards(): pl.pallas_call(write_out, out_shape=tuple((jax.ShapeDtypeStruct(s, d) for...  2.16 us

profile of v5, /device:TPU:1, one launch (start us, length us, event | category | flops | bytes accessed | tf_op | source)
XLA Modules:
  0.0 85.4 jit_solution(6498363000728914234)
XLA Ops:
  0.6 82.6 %shard_map.119 = (bf16[64,3584]{1,0:T(8,128)(2,1)S(1)}, f32[64,3584]{1,0:T(8,128)S(1)}, f32[512,512]{1,0:T(8,128)S(1)}, f32[512,512]{1,0:T(8,128)S(1)}, f32[512,512]{1,0:T(8,128)S(1)}) custom-call(s32[1,56]{1,0:T(1,128)} %tgt_hbm.1, bf16[64,3584]{1,0:T(8,128)(2,1)} %grad_hbm.1, f32[64,3584]{1,0:T(8,128)} %first_hbm.1, f32[512,512]{1,0:T(8,128)} %bitcast.8, ...), custom_call_target="tpu_custom_call" | custom-call | flops 2147483648 | bytes 12582912 | tf_op jit(solution)/shard_map/pallas_call | solution.py:686
  83.2 2.2 %shard_map.120 = (bf16[64,3584]{1,0:T(8,128)(2,1)}, f32[64,3584]{1,0:T(8,128)}, f32[512,512]{1,0:T(8,128)}, f32[512,512]{1,0:T(8,128)}, f32[512,512]{1,0:T(8,128)}) custom-call(bf16[64,3584]{1,0:T(8,128)(2,1)S(1)} %get-tuple-element.15.refs_0_, f32[64,3584]{1,0:T(8,128)S(1)} %get-tuple-element.16.refs_1_, f32[512,512]{1,0:T(8,128)S(1)} %get-tuple-element.17.refs_2_, ...), custom_call_target="tpu_custom_call" | custom-call | tf_op jit(solution)/shard_map/pallas_call | solution.py:760

commit v6 on v5

--- a/solution.py
+++ b/solution.py
@@ -444,13 +444,13 @@
                 lo = j * BLOCK + xx * LANE
                 out_v[r * RC : (r + 1) * RC, lo : lo + LANE] = uf[r, xx, j]
 
-    def uf_spread(upds):
+    def uf_spread(upd):
         for h in range(2):
             for xx in range(NX):
                 for cc in range(NC):
                     for i in range(HALF):
-                        lo = (i * NC + cc) * RC
-                        fub[xx, cc, h * HALF + i] = upds[h][
+                        lo = ((i * NC + cc) * 2 + h) * RC
+                        fub[xx, cc, h * HALF + i] = upd[
                             lo : lo + RC, xx * LANE : (xx + 1) * LANE
                         ]
         for dx, dc in near:
@@ -619,13 +619,13 @@
         mhalf = mm(qlt_v[...], blk[1].reshape(BLOCK, BLOCK)).astype(BF16)
         normed = (mm(mhalf, qr_v[...]) / den_v[...]).astype(BF16)
 
-    def update(r):
-        rows = ql_v[:, r * RC : (r + 1) * RC, :].reshape(HALF * NC * RC, BLOCK)
+    def update(r, n=1):
+        rows = ql_v[:, r * RC : (r + n) * RC, :].reshape(HALF * NC * n * RC, BLOCK)
         return mm(mm(rows, normed).astype(BF16), qrt_v[...]).astype(BF16)
 
     group[0] = 1
     d_exchange(0, update(0))
-    uf_spread([update(FOLD), update(FOLD + 1)])
+    uf_spread(update(FOLD, 2))
     upd = update(1)
 
     wait_units(sent[0], send_sem.at[0])

time: 85.5 us -> 85.4 us (level)
    pallas_call x1, Pallas kernels: 82.6 us -> 81.7 us  [shards(): pl.pallas_call(functools.partial(kernel, rows * cols * n_fsdp * n_mp), ou...]
where the time goes in v6:
time: 85.4 us; the launch traced here: 84.5 us
  Pallas kernels  83.9 us (98%)
    pallas_call x1, Pallas kernels, shards(): pl.pallas_call(functools.partial(kernel, rows * cols * n_fsdp * n_mp), ou...  81.7 us
    pallas_call x1, Pallas kernels, shards(): pl.pallas_call(write_out, out_shape=tuple((jax.ShapeDtypeStruct(s, d) for...  2.16 us

profile of v6, /device:TPU:1, one launch (start us, length us, event | category | flops | bytes accessed | tf_op | source)
XLA Modules:
  0.0 84.5 jit_solution(7895714918030437697)
XLA Ops:
  0.6 81.7 %shard_map.119 = (bf16[64,3584]{1,0:T(8,128)(2,1)S(1)}, f32[64,3584]{1,0:T(8,128)S(1)}, f32[512,512]{1,0:T(8,128)S(1)}, f32[512,512]{1,0:T(8,128)S(1)}, f32[512,512]{1,0:T(8,128)S(1)}) custom-call(s32[1,56]{1,0:T(1,128)} %tgt_hbm.1, bf16[64,3584]{1,0:T(8,128)(2,1)} %grad_hbm.1, f32[64,3584]{1,0:T(8,128)} %first_hbm.1, f32[512,512]{1,0:T(8,128)} %bitcast.8, ...), custom_call_target="tpu_custom_call" | custom-call | flops 2147483648 | bytes 12582912 | tf_op jit(solution)/shard_map/pallas_call | solution.py:686
  82.3 2.2 %shard_map.120 = (bf16[64,3584]{1,0:T(8,128)(2,1)}, f32[64,3584]{1,0:T(8,128)}, f32[512,512]{1,0:T(8,128)}, f32[512,512]{1,0:T(8,128)}, f32[512,512]{1,0:T(8,128)}) custom-call(bf16[64,3584]{1,0:T(8,128)(2,1)S(1)} %get-tuple-element.15.refs_0_, f32[64,3584]{1,0:T(8,128)S(1)} %get-tuple-element.16.refs_1_, f32[512,512]{1,0:T(8,128)S(1)} %get-tuple-element.17.refs_2_, ...), custom_call_target="tpu_custom_call" | custom-call | tf_op jit(solution)/shard_map/pallas_call | solution.py:760
